TPU v7x, 256 devices: a whole 4x4x8 slice. The times are simulated.
256 devices in a mesh: wide: 64 (over x, z, core), narrow: 4 (over y).
Axes of the slice: x: 4, y: 4, z: 8, core: 2. Of those that a mesh axis runs over, the one named last changes fastest.
Arguments:
- potentials: float32 [64, 128, 128, 128], P('wide', 'narrow'), may hold values from -190 to 190
- parents: int32 [64], replicated, may hold values from 0 to 20, as said below
- separator_excluded: int32 [64], replicated, may hold values from 0 to 2
- measurement_clique: int32 [64], replicated, may hold values from 0 to 63, as said below
- measured: float32 [64, 128, 128], P('wide', 'narrow'), may hold values from 0.25 to 4
Outputs:
- marginal: float32 [64, 128, 128], P('wide', 'narrow')
- updated: float32 [64, 128, 128, 128], P('wide', 'narrow')
Inputs may be any that keep to these rules, and one draw needn't show every extreme that they name: parents[0] = 0; a clique c with 1 <= c < 5 has parent 0, one with 5 <= c < 21 a parent in 1 to 4, and one with c >= 21 a parent in 5 to 20; the last clique has parent 21 - 1. `measurement_clique`: every clique is named by exactly one measured marginal.
All inputs are finite; a program needn't handle non-finite values.
Results may differ from a plain program's by a relative error of at most 0.0003.
Values sent between devices are 32-bit elements; how exact they have to be, the bound alone decides.
A program may use at most 64 MiB of HBM per device.

v0:
```python
import jax
import jax.numpy as jnp
from jax import lax
from jax.sharding import PartitionSpec as P

DEPTH = 3


def merged_2(part, axis, combine):
    gathered = jax.tree.map(lambda a: lax.all_gather(a, axis), part)

    def take(source):
        return jax.tree.map(lambda a: lax.dynamic_index_in_dim(a, source, 0, False), gathered)

    return lax.fori_loop(
        1, lax.axis_size(axis), lambda source, state: combine(state, take(source)), take(0)
    )


def log_sum(values, along):
    largest_entry = jnp.max(values, axis=along, keepdims=True)
    return jnp.squeeze(largest_entry, along) + jnp.log(
        jnp.sum(jnp.exp(values - largest_entry), axis=along)
    )


def join_tables(first, second):
    largest_entry = jnp.maximum(first[0], second[0])
    return (
        largest_entry,
        first[1] * jnp.exp(first[0] - largest_entry)
        + second[1] * jnp.exp(second[0] - largest_entry),
    )


def outgoing(belief, quarter_index, rows_here):
    largest_entry = jnp.max(belief, axis=0)
    summed = jnp.sum(jnp.exp(belief - largest_entry[None]), axis=0)
    merged = merged_2((largest_entry, summed), "narrow", join_tables)
    drop_first = merged[0] + jnp.log(merged[1])
    drop_first = lax.dynamic_slice_in_dim(drop_first, quarter_index * rows_here, rows_here, 0)
    return jnp.stack([drop_first, log_sum(belief, 1), log_sum(belief, 2)])


def body(potentials, parents, separator_excluded, measurement_clique, measured):
    own_slab = potentials[0]
    rows_here = own_slab.shape[0]
    domain = own_slab.shape[2]
    wide_count = lax.axis_size("wide")
    self_index = lax.axis_index("wide")
    quarter_index = lax.axis_index("narrow")
    first_leaf = 1 + max(1, wide_count // 16) + wide_count // 4
    parent_row = parents[self_index]
    kind_row = separator_excluded[self_index]
    belief = own_slab
    for iteration in range(DEPTH):
        tables = outgoing(belief, quarter_index, rows_here)
        gathered = lax.all_gather(tables[None], "wide", axis=0, tiled=True)
        picked = gathered[parent_row, kind_row]
        complete = lax.all_gather(picked, "narrow", axis=0, tiled=True)
        complete = jnp.where(self_index > 0, complete, jnp.float32(0.0))
        belief = own_slab + complete[None]
    scale = jnp.float32(domain * domain)
    largest_entry = jnp.max(belief)
    summed = jnp.sum(jnp.exp(belief - largest_entry))
    merged = merged_2((largest_entry, summed), "narrow", join_tables)
    logz = merged[0] + jnp.log(merged[1])
    weighted = scale * jnp.sum(jnp.exp(belief - logz), axis=0)
    marginal = lax.psum_scatter(weighted, "narrow", scatter_dimension=0, tiled=True)
    source_row = jnp.sum(
        jnp.where(
            measurement_clique == self_index,
            jnp.arange(measurement_clique.shape[0], dtype=jnp.int32),
            0,
        )
    )
    pieces = lax.all_gather(measured, "wide", axis=0, tiled=True)
    row_ids = jnp.arange(pieces.shape[0], dtype=jnp.int32)
    selector = (row_ids == source_row).astype(jnp.float32)
    own_measure = jnp.einsum("m,mqk->qk", selector, pieces, precision=lax.Precision.HIGHEST)
    residual = marginal - own_measure
    residual_whole = lax.all_gather(residual, "narrow", axis=0, tiled=True)
    step_term = jnp.where(self_index >= first_leaf, residual_whole, jnp.float32(0.0))
    updated = own_slab - jnp.float32(0.5) * step_term[None]
    return (marginal[None], updated[None])


def solution(mesh):
    return jax.shard_map(
        body,
        mesh=mesh,
        in_specs=(P("wide", "narrow", None, None), P(), P(), P(), P("wide", "narrow", None)),
        out_specs=(P("wide", "narrow", None), P("wide", "narrow", None, None)),
        check_vma=False,
    )
```

profile of v0, /device:TPU:7, one launch (start us, length us, event | category | flops | bytes accessed | tf_op | source)
XLA Modules:
  0.0 465.3 jit_solution(12748854386773682030)
XLA Ops:
  7.2 2.4 fusion.29
  9.6 10.4 %all-gather = f32[512,128]{1,0:T(8,128)S(1)} all-gather(f32[128,128]{1,0:T(8,128)S(1)} %get-tuple-element.555), channel_id=2, replica_groups=mesh['wide'=64,'narrow'=4] {'narrow'}, dimensions={0}, use_global_device_ids=true | all-gather | bytes 327680 | tf_op jit(solution)/shard_map/all_gather | solution.py:10
  20.0 1.5 fusion.7
  21.5 9.4 %all-gather.1 = f32[512,128]{1,0:T(8,128)S(1)} all-gather(f32[128,128]{1,0:T(8,128)S(1)} %get-tuple-element.552), channel_id=3, replica_groups=mesh['wide'=64,'narrow'=4] {'narrow'}, dimensions={0}, use_global_device_ids=true | all-gather | bytes 327680 | tf_op jit(solution)/shard_map/all_gather | solution.py:10
  30.9 0.3 while.68
  30.9 0.1 fusion.33
  31.0 0.1 fusion.33
  31.1 0.1 fusion.33
  31.2 0.6 pad_maximum_fusion
  31.9 0.0 all-gather.21.cloned.1.call-start
  32.0 0.6 dynamic_slice.133
  33.9 0.6 dynamic_slice.134
  37.0 80.1 %all-gather.19.cloned.1.call-done = f32[192,32,128]{2,1,0:T(8,128)} async-done(((f32[3,32,128]{2,1,0:T(8,128)}), f32[192,32,128]{2,1,0:T(8,128)}) %all-gather.19.cloned.1.call-update) | async-done | bytes 3145744 | tf_op jit(solution)/shard_map/all_gather | solution.py:58
  117.1 0.7 constant_dynamic-slice_fusion.2
  117.8 9.6 %all-gather.3 = f32[1,1,128,128]{3,2,1,0:T(8,128)S(1)} all-gather(f32[1,1,32,128]{3,2,1,0:T(8,128)S(1)} %constant_dynamic-slice_fusion.2), channel_id=5, replica_groups=mesh['wide'=64,'narrow'=4] {'narrow'}, dimensions={2}, use_global_device_ids=true | all-gather | bytes 81920 | tf_op jit(solution)/shard_map/all_gather | solution.py:60
  127.4 0.2 fusion.15
  127.6 0.6 exponential_reduce_fusion.7
  128.3 9.4 %all-gather.4 = f32[512,128]{1,0:T(8,128)S(1)} all-gather(f32[128,128]{1,0:T(8,128)S(1)} %fusion.15), channel_id=6, replica_groups=mesh['wide'=64,'narrow'=4] {'narrow'}, dimensions={0}, use_global_device_ids=true | all-gather | bytes 327680 | tf_op jit(solution)/shard_map/all_gather | solution.py:10
  137.6 9.4 %all-gather.5 = f32[512,128]{1,0:T(8,128)S(1)} all-gather(f32[128,128]{1,0:T(8,128)S(1)} %get-tuple-element.547), channel_id=7, replica_groups=mesh['wide'=64,'narrow'=4] {'narrow'}, dimensions={0}, use_global_device_ids=true | all-gather | bytes 327680 | tf_op jit(solution)/shard_map/all_gather | solution.py:10
  147.0 0.3 while.69
  147.0 0.1 fusion.34
  147.1 0.1 fusion.34
  147.2 0.1 fusion.34
  147.3 1.3 exponential_reduce_fusion.6
  148.7 0.6 pad_maximum_fusion.1
  149.4 83.6 %all-gather.21.cloned.1.call-done = f32[192,32,128]{2,1,0:T(8,128)} async-done(((f32[3,32,128]{2,1,0:T(8,128)}), f32[192,32,128]{2,1,0:T(8,128)}) %all-gather.21.cloned.1.call-update) | async-done | bytes 3145744 | tf_op jit(solution)/shard_map/all_gather | solution.py:58
  233.0 0.7 constant_dynamic-slice_fusion.1
  233.7 9.6 %all-gather.7 = f32[1,1,128,128]{3,2,1,0:T(8,128)S(1)} all-gather(f32[1,1,32,128]{3,2,1,0:T(8,128)S(1)} %constant_dynamic-slice_fusion.1), channel_id=9, replica_groups=mesh['wide'=64,'narrow'=4] {'narrow'}, dimensions={2}, use_global_device_ids=true | all-gather | bytes 81920 | tf_op jit(solution)/shard_map/all_gather | solution.py:60
  243.4 0.2 fusion.18
  243.6 0.6 exponential_reduce_fusion.4
  244.2 9.4 %all-gather.8 = f32[512,128]{1,0:T(8,128)S(1)} all-gather(f32[128,128]{1,0:T(8,128)S(1)} %fusion.18), channel_id=10, replica_groups=mesh['wide'=64,'narrow'=4] {'narrow'}, dimensions={0}, use_global_device_ids=true | all-gather | bytes 327680 | tf_op jit(solution)/shard_map/all_gather | solution.py:10
  253.6 9.4 %all-gather.9 = f32[512,128]{1,0:T(8,128)S(1)} all-gather(f32[128,128]{1,0:T(8,128)S(1)} %get-tuple-element.542), channel_id=11, replica_groups=mesh['wide'=64,'narrow'=4] {'narrow'}, dimensions={0}, use_global_device_ids=true | all-gather | bytes 327680 | tf_op jit(solution)/shard_map/all_gather | solution.py:10
  263.0 0.3 while.70
  263.0 0.1 fusion.35
  263.1 0.1 fusion.35
  263.2 0.1 fusion.35
  263.2 1.3 exponential_reduce_fusion.3
  264.6 0.6 pad_maximum_fusion.2
  265.3 0.5 all-gather.17.cloned.1.call-update
  265.9 0.6 dynamic-slice
  266.6 0.6 fusion.26
  267.2 81.8 %all-gather.23.cloned.1.call-done = f32[192,32,128]{2,1,0:T(8,128)} async-done(((f32[3,32,128]{2,1,0:T(8,128)}), f32[192,32,128]{2,1,0:T(8,128)}) %all-gather.23.cloned.1.call-update) | async-done | bytes 3145744 | tf_op jit(solution)/shard_map/all_gather | solution.py:58
  349.0 0.7 constant_dynamic-slice_fusion
  349.7 9.6 %all-gather.11 = f32[1,1,128,128]{3,2,1,0:T(8,128)S(1)} all-gather(f32[1,1,32,128]{3,2,1,0:T(8,128)S(1)} %constant_dynamic-slice_fusion), channel_id=13, replica_groups=mesh['wide'=64,'narrow'=4] {'narrow'}, dimensions={2}, use_global_device_ids=true | all-gather | bytes 81920 | tf_op jit(solution)/shard_map/all_gather | solution.py:60
  359.3 1.2 fusion.12
  360.5 1.9 exponential_reduce_fusion.1
  362.3 1.4 dynamic-update-slice.1
  363.8 1.4 dynamic-update-slice
  365.1 7.8 %all-reduce.2 = (f32[4]{0:T(128)S(1)}, f32[4]{0:T(128)S(1)}) all-reduce(f32[4]{0:T(128)S(1)} %dynamic-update-slice, f32[4]{0:T(128)S(1)} %dynamic-update-slice.1), channel_id=1, replica_groups=mesh['wide'=64,'narrow'=4] {'narrow'}, use_global_device_ids=true, to_apply=%add | all-reduce | flops 8 | bytes 64
  373.0 9.7 %while.71 = (s32[]{:T(128)}, f32[]{:T(128)}, f32[]{:T(128)}, f32[4]{0:T(128)S(1)}, f32[4]{0:T(128)S(1)}, /*index=5*/s32[]{:T(128)}, s32[]{:T(128)}, s32[]{:T(128)}) while((s32[]{:T(128)}, f32[]{:T(128)}, f32[]{:T(128)}, f32[4]{0:T(128)S(1)}, f32[4]{0:T(128)S(1)}, /*index=5*/s32[]{:T(128)}, s32[]{:T(128)}, s32[]{:T(128)}) %tuple.162), condition=%wide.region_27.28_spmd, body=%wide.region_26.27_spmd.sunk | while | flops 11 | bytes 247 | solution.py:15
  373.0 0.6 dynamic_slice.193
  374.9 0.6 dynamic_slice.194
  376.2 0.6 dynamic_slice.193
  378.1 0.6 dynamic_slice.194
  379.5 0.6 dynamic_slice.193
  381.4 0.6 dynamic_slice.194
  382.7 0.4 exponential_reduce_fusion
  383.1 0.6 broadcast_multiply_fusion
  383.7 42.0 %all-gather.17.cloned.1.call-done = f32[64,32,128]{2,1,0:T(8,128)} async-done(((f32[1,32,128]{2,1,0:T(8,128)}), f32[64,32,128]{2,1,0:T(8,128)}) %all-gather.17.cloned.1.call-update) | async-done | bytes 1048592 | tf_op jit(solution)/shard_map/all_gather | solution.py:77
  425.7 2.8 fusion.19
  428.5 19.0 %reduce-scatter.2.cloned.1.call-done = f32[32,128]{1,0:T(8,128)} async-done(((f32[128,128]{1,0:T(8,128)}), f32[32,128]{1,0:T(8,128)}) %reduce-scatter.2.cloned.1.call-update) | async-done | bytes 16400 | tf_op jit(solution)/shard_map/reduce_scatter | solution.py:69
  447.5 0.7 sub.198
  448.3 9.0 %all_gather.95 = f32[128,128]{1,0:T(8,128)S(1)} all-gather(f32[32,128]{1,0:T(8,128)S(1)} %sub.198), channel_id=1, replica_groups=mesh['wide'=64,'narrow'=4] {'narrow'}, dimensions={0}, use_global_device_ids=true | all-gather | bytes 81920 | tf_op jit(solution)/shard_map/all_gather | solution.py:82
  457.2 1.6 broadcast_subtract_fusion
  (38 shorter events, 0.4 us)
Async XLA Ops:
  7.2 12.8 %copy-start = (f32[1,32,128,128]{3,2,1,0:T(8,128)S(1)}, f32[1,32,128,128]{3,2,1,0:T(8,128)}, u32[]{:S(2)}) copy-start(f32[1,32,128,128]{3,2,1,0:T(8,128)} %param.13) | copy-start | bytes 6291460
  7.2 109.9 %all-gather.19.cloned.1.call-start = ((), (), s32[]{:S(2)}) async-start(), calls=%async_computation.3 | async-start | bytes 3194880 | tf_op jit(solution)/shard_map/all_gather | solution.py:58
  21.5 10.4 %copy-start.1 = (s32[64]{0:T(128)S(1)}, s32[64]{0:T(128)}, u32[]{:S(2)}) copy-start(s32[64]{0:T(128)} %param.14) | copy-start | bytes 772
  21.5 12.3 %copy-start.2 = (s32[64]{0:T(128)S(1)}, s32[64]{0:T(128)}, u32[]{:S(2)}) copy-start(s32[64]{0:T(128)} %param.15) | copy-start | bytes 772
  31.9 201.1 %all-gather.21.cloned.1.call-start = ((), (), s32[]{:S(2)}) async-start(), calls=%async_computation.4 | async-start | bytes 3194880 | tf_op jit(solution)/shard_map/all_gather | solution.py:58
  149.3 199.6 %all-gather.23.cloned.1.call-start = ((), (), s32[]{:S(2)}) async-start(), calls=%async_computation.5 | async-start | bytes 3194880 | tf_op jit(solution)/shard_map/all_gather | solution.py:58
  262.9 3.0 copy-start.4
  263.0 3.6 copy-start.3
  265.3 160.4 %all-gather.17.cloned.1.call-start = ((), (), s32[]{:S(2)}) async-start(), calls=%async_computation.2 | async-start | bytes 1064960 | tf_op jit(solution)/shard_map/all_gather | solution.py:77
  265.9 181.7 %reduce-scatter.2.cloned.1.call-start = ((), (), s32[]{:S(2)}) async-start(), calls=%async_computation.1 | async-start | bytes 81920 | tf_op jit(solution)/shard_map/reduce_scatter | solution.py:69
Sparse Core Ops, SparseCore 0:
  32.0 85.0 all-gather.18
  149.5 83.5 all-gather.20
  265.4 83.5 all-gather.22
  351.6 74.0 all-gather.16
  428.6 18.8 reduce-scatter.1
where the time goes:
time: 471 us; the launch traced here: 465 us
  waiting for transfers between devices  307 us (65%)
  blocking collectives  103 us (22%)
  between operations  18 us (4%)
  other arithmetic  17.7 us (4%)
  local copies, waits for them, and re-layouts  10.3 us (2%)
  loops' own time  6.39 us (1%)
    all_gather x3, waiting for transfers between devices, body(): gathered = lax.all_gather(tables[None], 'wide', axis=0, tiled=True)  246 us
    all_gather x6, blocking collectives, merged_2(): gathered = jax.tree.map(lambda a: lax.all_gather(a, axis), part)  57.2 us
    all_gather x1, waiting for transfers between devices, body(): pieces = lax.all_gather(measured, 'wide', axis=0, tiled=True)  42 us
    all_gather x3, blocking collectives, body(): complete = lax.all_gather(picked, 'narrow', axis=0, tiled=True)  28.9 us
    reduce_scatter x1, waiting for transfers between devices, body(): lax.psum_scatter(weighted, 'narrow', scatter_dimension=0, tiled=True)  19 us
  transfers between devices with their start and end apart: 5, of which 5 were waited for; matrix products, arithmetic and copies ran while one was open for 4% of the time, Pallas kernels for 0%

commit v1 on v0

v1 whole, which is shorter than its diff:
```python
import jax
import jax.numpy as jnp
from jax import lax
from jax.experimental import pallas as pl
from jax.experimental.pallas import tpu as pltpu
from jax.sharding import PartitionSpec as P

MESH = pl.DeviceIdType.MESH
K = 128
QUARTERS = 4
ROWS = K // QUARTERS
CLIQUES = 64
LEVEL1, LEVEL2 = 5, 21
FIRST = LEVEL1 - 1
SECOND = LEVEL2 - LEVEL1
LEAVES = CLIQUES - LEVEL2
SUB = ROWS // SECOND


def sweep_kernel(
    parents, kinds, targets, pot, measured, out,
    partial, partial_in, own_l0, message, message_t, pot_t, top, total, tables,
    to_first, to_second, candidates, sub_tables, relay_tables,
    sub_measured, relay_measured, to_leaf, from_relay, final,
    sem_l0, sem_first, sem_second, sem_rows, sem_relay, sem_measured, sem_leaf, sem_final,
):
    me = lax.axis_index("wide")
    quarter = lax.axis_index("narrow")
    is_root = me == 0
    is_first = jnp.logical_and(me >= 1, me < LEVEL1)
    is_second = jnp.logical_and(me >= LEVEL1, me < LEVEL2)
    is_leaf = me >= LEVEL2
    is_inner = me < LEVEL2

    def peer(step):
        return lax.rem(quarter + step, QUARTERS)

    def repeat(count, function):
        def run(index, carry):
            function(index)
            return carry

        lax.fori_loop(0, count, run, 0)

    def send(source, target, sem, device):
        pltpu.make_async_remote_copy(
            src_ref=source, dst_ref=target, send_sem=sem.at[0], recv_sem=sem.at[1],
            device_id=device, device_id_type=MESH,
        ).start()

    def await_bytes(like, sem, which):
        pltpu.make_async_copy(like, like, sem.at[which]).wait()

    barrier = pltpu.get_barrier_semaphore()

    def greet(wide, narrow):
        pl.semaphore_signal(barrier, inc=1, device_id=(wide, narrow), device_id_type=MESH)

    for step in range(1, QUARTERS):
        greet(me, peer(step))

    @pl.when(is_first)
    def _():
        for other in range(QUARTERS):
            greet(0, other)

    @pl.when(is_second)
    def _():
        def one(step):
            greet(lax.rem(me + 1 + step, CLIQUES), quarter)

        repeat(CLIQUES - 1, one)

    @pl.when(is_leaf)
    def _():
        repeat(SECOND, lambda relay: greet(LEVEL1 + relay, quarter))

    for relay in range(SECOND):
        sub_measured[relay] = measured[relay * SUB:(relay + 1) * SUB, :]

    def partial_lse(block):
        rows = pl.ds(pl.multiple_of(block * 8, 8), 8)
        slab = pot[:, rows, :]
        largest = jnp.max(slab, axis=0)
        partial[rows, :] = largest + jnp.log(jnp.sum(jnp.exp(slab - largest[None]), axis=0))

    repeat(K // 8, partial_lse)

    peers = QUARTERS - 1

    @pl.when(is_root)
    def _():
        pl.semaphore_wait(barrier, peers + SECOND + FIRST * QUARTERS)

    @pl.when(jnp.logical_or(is_first, is_leaf))
    def _():
        pl.semaphore_wait(barrier, peers + SECOND)

    @pl.when(is_second)
    def _():
        pl.semaphore_wait(barrier, peers + SECOND - 1 + LEAVES)

    for step in range(1, QUARTERS):
        rows = pl.ds(pl.multiple_of(peer(step) * ROWS, ROWS), ROWS)
        send(partial.at[rows], partial_in.at[step - 1], sem_l0, (me, peer(step)))

    def give_measured(relay):
        @pl.when(me != LEVEL1 + relay)
        def _():
            send(sub_measured.at[relay], relay_measured.at[me], sem_measured, (LEVEL1 + relay, quarter))

    repeat(SECOND, give_measured)

    @pl.when(is_inner)
    def _():
        def turn(a0):
            pot_t[a0] = pot[a0].T

        repeat(ROWS, turn)

    @pl.when(is_root)
    def _():
        message[...] = jnp.zeros_like(message)

    @pl.when(is_first)
    def _():
        await_bytes(message, sem_first, 1)

    @pl.when(is_second)
    def _():
        await_bytes(candidates, sem_second, 1)
        message[quarter] = candidates[jnp.maximum(parents[me] - 1, 0)]
        for step in range(1, QUARTERS):
            send(message.at[quarter], message.at[quarter], sem_rows, (me, peer(step)))
        await_bytes(message.at[pl.ds(0, QUARTERS - 1)], sem_rows, 1)

    @pl.when(is_inner)
    def _():
        for other in range(QUARTERS):
            message_t[:, other * ROWS:(other + 1) * ROWS] = message[other].T

        def reduce_rows(a0):
            row = pl.ds(a0, 1)
            for kind in (1, 2):
                if kind == 1:
                    belief = pot[a0].reshape(QUARTERS, ROWS, K) + message[...]
                    belief = belief.reshape(K, K)
                else:
                    belief = pot_t[a0] + message_t[...]
                largest = jnp.max(belief, axis=0, keepdims=True)
                top[kind - 1, row, :] = largest
                total[kind - 1, row, :] = jnp.sum(jnp.exp(belief - largest), axis=0, keepdims=True)

        repeat(ROWS, reduce_rows)
        for kind in (1, 2):
            tables[kind] = top[kind - 1] + jnp.log(total[kind - 1])

    await_bytes(partial_in, sem_l0, 1)
    mine = partial[pl.ds(pl.multiple_of(quarter * ROWS, ROWS), ROWS), :]
    largest = jnp.maximum(mine, jnp.max(partial_in[...], axis=0))
    summed = jnp.exp(mine - largest) + jnp.sum(jnp.exp(partial_in[...] - largest[None]), axis=0)
    own_l0[...] = largest + jnp.log(summed)

    @pl.when(is_inner)
    def _():
        tables[0] = own_l0[...] + message[quarter]
        final[0] = tables[0]
        final[1] = jnp.zeros_like(final[1])

    @pl.when(is_root)
    def _():
        for child in range(FIRST):
            to_first[child] = tables[kinds[1 + child]]
            for other in range(QUARTERS):
                send(to_first.at[child], message.at[quarter], sem_first, (1 + child, other))

    @pl.when(is_first)
    def _():
        def give(child):
            to_second[child] = tables[kinds[LEVEL1 + child]]
            send(to_second.at[child], candidates.at[me - 1], sem_second, (LEVEL1 + child, quarter))

        repeat(SECOND, give)

    @pl.when(is_second)
    def _():
        slot = me - LEVEL1
        for kind in range(3):
            for relay in range(SECOND):
                sub_tables[relay, kind] = tables[kind, relay * SUB:(relay + 1) * SUB, :]

        def give_tables(relay):
            @pl.when(slot != relay)
            def _():
                send(sub_tables.at[relay], relay_tables.at[slot], sem_relay, (LEVEL1 + relay, quarter))

        repeat(SECOND, give_tables)
        relay_tables[slot] = sub_tables[slot]
        await_bytes(relay_measured.at[pl.ds(0, CLIQUES - 1)], sem_measured, 1)
        relay_measured[me] = sub_measured[slot]
        clique = lax.broadcasted_iota(jnp.int32, (CLIQUES, CLIQUES), 0)
        chosen = (clique == targets[...]).astype(jnp.float32)
        for row in range(SUB):
            to_leaf[:, 1, row, :] = jnp.dot(
                chosen, relay_measured[:, row, :],
                precision=lax.Precision.HIGHEST, preferred_element_type=jnp.float32,
            )
        await_bytes(relay_tables.at[pl.ds(0, SECOND - 1)], sem_relay, 1)

        def give_leaf(leaf):
            child = LEVEL2 + leaf
            to_leaf[child, 0] = relay_tables[jnp.maximum(parents[child] - LEVEL1, 0), kinds[child]]
            send(to_leaf.at[child], from_relay.at[slot], sem_leaf, (child, quarter))

        repeat(LEAVES, give_leaf)

    @pl.when(is_leaf)
    def _():
        await_bytes(from_relay, sem_leaf, 1)
        for relay in range(SECOND):
            rows = slice(relay * SUB, (relay + 1) * SUB)
            final[0, rows, :] = own_l0[rows, :] + from_relay[relay, 0]
            final[1, rows, :] = from_relay[relay, 1]

    for step in range(1, QUARTERS):
        send(final, out.at[quarter], sem_final, (me, peer(step)))
    out[quarter] = final[...]
    await_bytes(out.at[pl.ds(0, QUARTERS - 1)], sem_final, 1)

    await_bytes(partial_in, sem_l0, 0)
    await_bytes(out.at[pl.ds(0, QUARTERS - 1)], sem_final, 0)

    @pl.when(is_root)
    def _():
        for _ in range(QUARTERS):
            await_bytes(to_first, sem_first, 0)

    @pl.when(is_first)
    def _():
        await_bytes(to_second, sem_second, 0)

    @pl.when(is_second)
    def _():
        await_bytes(message.at[pl.ds(0, QUARTERS - 1)], sem_rows, 0)
        await_bytes(relay_tables.at[pl.ds(0, SECOND - 1)], sem_relay, 0)
        await_bytes(relay_measured.at[pl.ds(0, SECOND - 1)], sem_measured, 0)
        await_bytes(to_leaf.at[pl.ds(0, LEAVES)], sem_leaf, 0)

    @pl.when(jnp.logical_not(is_second))
    def _():
        await_bytes(sub_measured, sem_measured, 0)


def sweep(parents, kinds, targets, pot, measured):
    vmem, smem = pl.BlockSpec(memory_space=pltpu.VMEM), pl.BlockSpec(memory_space=pltpu.SMEM)
    f32 = jnp.float32
    scratch = [
        (K, K), (QUARTERS - 1, ROWS, K), (ROWS, K), (QUARTERS, ROWS, K), (K, K), (ROWS, K, K),
        (2, ROWS, K), (2, ROWS, K), (3, ROWS, K),
        (FIRST, ROWS, K), (SECOND, ROWS, K), (FIRST, ROWS, K), (SECOND, 3, SUB, K), (SECOND, 3, SUB, K),
        (SECOND, SUB, K), (CLIQUES, SUB, K), (CLIQUES, 2, SUB, K), (SECOND, 2, SUB, K), (2, ROWS, K),
    ]
    return pl.pallas_call(
        sweep_kernel,
        out_shape=jax.ShapeDtypeStruct((QUARTERS, 2, ROWS, K), f32),
        in_specs=[smem, smem, vmem, vmem, vmem],
        out_specs=vmem,
        scratch_shapes=[pltpu.VMEM(shape, f32) for shape in scratch] + [pltpu.SemaphoreType.DMA((2,))] * 8,
        compiler_params=pltpu.CompilerParams(
            collective_id=0, has_side_effects=True, vmem_limit_bytes=24 * 1024 * 1024
        ),
        name="sweep",
    )(parents, kinds, targets, pot, measured)


BLOCK = 8


def finish_kernel(final, pot, marginal, updated, term):
    me = lax.axis_index("wide")
    quarter = lax.axis_index("narrow")

    @pl.when(pl.program_id(0) == 0)
    def _():
        cells = final[:, 0]
        largest = jnp.max(cells)
        weights = jnp.exp(cells - largest)
        scale = jnp.float32(K * K) / jnp.sum(weights)
        whole = weights * scale
        residual = whole - final[:, 1]
        term[...] = jnp.where(me >= LEVEL2, jnp.float32(0.5) * residual, jnp.float32(0.0))
        own = final[quarter, 0]
        marginal[...] = jnp.exp(own - largest) * scale

    for other in range(QUARTERS):
        rows = slice(other * ROWS, (other + 1) * ROWS)
        updated[:, rows, :] = pot[:, rows, :] - term[other][None]


def finish(final, pot):
    return pl.pallas_call(
        finish_kernel,
        grid=(ROWS // BLOCK,),
        out_shape=(
            jax.ShapeDtypeStruct((ROWS, K), jnp.float32),
            jax.ShapeDtypeStruct((ROWS, K, K), jnp.float32),
        ),
        in_specs=[
            pl.BlockSpec((QUARTERS, 2, ROWS, K), lambda i: (0, 0, 0, 0)),
            pl.BlockSpec((BLOCK, K, K), lambda i: (i, 0, 0)),
        ],
        out_specs=(
            pl.BlockSpec((ROWS, K), lambda i: (0, 0)),
            pl.BlockSpec((BLOCK, K, K), lambda i: (i, 0, 0)),
        ),
        scratch_shapes=[pltpu.VMEM((QUARTERS, ROWS, K), jnp.float32)],
        name="finish",
    )(final, pot)


def body(potentials, parents, separator_excluded, measurement_clique, measured):
    pot = potentials[0]
    final = sweep(parents, separator_excluded, measurement_clique[None], pot, measured[0])
    marginal, updated = finish(final, pot)
    return marginal[None], updated[None]


def solution(mesh):
    return jax.shard_map(
        body,
        mesh=mesh,
        in_specs=(P("wide", "narrow", None, None), P(), P(), P(), P("wide", "narrow", None)),
        out_specs=(P("wide", "narrow", None), P("wide", "narrow", None, None)),
        check_vma=False,
    )
```

time: 471 us -> 58.5 us (0.12); the launches traced: 465 us -> 57.7 us
  waiting for transfers between devices: 307 us -> 0 us
  blocking collectives: 103 us -> 0 us
  Pallas kernels: 0 us -> 52.1 us
  other arithmetic: 17.7 us -> 0 us
  between operations: 18 us -> 0.66 us
  loops' own time: 6.39 us -> 0 us
  local copies, waits for them, and re-layouts: 10.3 us -> 4.91 us
    all_gather x4 -> x0, waiting for transfers between devices: 287 us -> none  [the longest x3 246 us: body(): gathered = lax.all_gather(tables[None], 'wide', axis=0, tiled=True)]
    all_gather x10 -> x0, blocking collectives: 95.1 us -> none  [the longest x6 57.2 us: merged_2(): gathered = jax.tree.map(lambda a: lax.all_gather(a, axis), part)]
    pallas_call x0 -> x2, Pallas kernels: none -> 52.1 us  [the longest x1 48 us: sweep(): pl.pallas_call(sweep_kernel, out_shape=jax.ShapeDtypeStruct((QUARTERS, 2,...]
    reduce_scatter x1 -> x0, waiting for transfers between devices: 19 us -> none  [body(): lax.psum_scatter(weighted, 'narrow', scatter_dimension=0, tiled=True)]
    reduce_sum x8 -> x0, other arithmetic: 8.32 us -> none  [the longest x3 2.77 us: outgoing(): summed = jnp.sum(jnp.exp(belief - largest_entry[None]), axis=0)]
    unnamed x1 -> x0, blocking collectives: 7.77 us -> none
    dynamic_slice x17 -> x0, local copies, waits for them, and re-layouts: 6.9 us -> none  [the longest x12 3.56 us: take(): lax.dynamic_index_in_dim(a, source, 0, False)]
    another operation x4 -> x0, loops' own time: 6.39 us -> none  [merged_2(): lax.fori_loop(1, lax.axis_size(axis), lambda source, state: combine(state...]
  transfers between devices with their start and end apart: 5 -> 0, of which waited for: 5 -> 0; matrix products, arithmetic and copies ran while one was open for 4% -> 0% of each run, Pallas kernels for 0% -> 0%
where the time goes in v1:
time: 58.5 us; the launch traced here: 57.7 us
  Pallas kernels  52.1 us (89%)
  local copies, waits for them, and re-layouts  4.91 us (8%)
  between operations  0.66 us (1%)
    pallas_call x1, Pallas kernels, sweep(): pl.pallas_call(sweep_kernel, out_shape=jax.ShapeDtypeStruct((QUARTERS, 2,...  48 us
    unnamed x12, local copies, waits for them, and re-layouts  4.91 us
    pallas_call x1, Pallas kernels, finish(): pl.pallas_call(finish_kernel, grid=(ROWS // BLOCK,), out_shape=(jax.Shape...  4.12 us

profile of v1, /device:TPU:7, one launch (start us, length us, event | category | flops | bytes accessed | tf_op | source)
XLA Modules:
  0.0 57.7 jit_solution(3493955285369374180)
XLA Ops:
  0.6 0.0 copy-start
  0.6 1.6 %copy-done = f32[1,32,128,128]{3,2,1,0:T(8,128)S(1)} copy-done((f32[1,32,128,128]{3,2,1,0:T(8,128)S(1)}, f32[1,32,128,128]{3,2,1,0:T(8,128)}, u32[]{:S(2)}) %copy-start) | copy-done | bytes 2097176
  2.2 0.0 copy-start.2
  2.2 0.7 %copy-done.2 = f32[1,32,128]{2,1,0:T(8,128)S(1)} copy-done((f32[1,32,128]{2,1,0:T(8,128)S(1)}, f32[1,32,128]{2,1,0:T(8,128)}, u32[]{:S(2)}) %copy-start.2) | copy-done | bytes 16408
  2.9 0.0 copy-start.3
  2.9 0.7 %copy-done.3 = s32[64]{0:T(128)S(1)} copy-done((s32[64]{0:T(128)S(1)}, s32[64]{0:T(128)}, u32[]{:S(2)}) %copy-start.3) | copy-done | bytes 280
  3.6 0.0 copy-start.4
  3.6 0.7 %copy-done.4 = s32[64]{0:T(128)S(1)} copy-done((s32[64]{0:T(128)S(1)}, s32[64]{0:T(128)}, u32[]{:S(2)}) %copy-start.4) | copy-done | bytes 280
  4.3 0.0 copy-start.5
  4.3 0.7 %copy-done.5 = s32[64]{0:T(128)S(1)} copy-done((s32[64]{0:T(128)S(1)}, s32[64]{0:T(128)}, u32[]{:S(2)}) %copy-start.5) | copy-done | bytes 280
  4.9 48.0 %sweep.1.final = f32[4,2,32,128]{3,2,1,0:T(8,128)S(1)} custom-call(s32[64]{0:T(128)S(1)} %copy-done.3, s32[64]{0:T(128)S(1)} %copy-done.4, s32[1,64]{1,0:T(1,128)S(1)} %bitcast.8, f32[32,128,128]{2,1,0:T(8,128)S(1)} %bitcast.6, f32[32,128]{1,0:T(8,128)S(1)} %bitcast.7), custom_call_target="tpu_custom_call" | custom-call | tf_op jit(solution)/shard_map/sweep/pallas_call | solution.py:263
  52.9 0.0 copy-start.1
  52.9 0.6 %copy-done.1 = f32[4,2,32,128]{3,2,1,0:T(8,128)} copy-done((f32[4,2,32,128]{3,2,1,0:T(8,128)}, f32[4,2,32,128]{3,2,1,0:T(8,128)S(1)}, u32[]{:S(2)}) %copy-start.1) | copy-done | bytes 131096
  53.6 4.1 %finish.1 = (f32[32,128]{1,0:T(8,128)}, f32[32,128,128]{2,1,0:T(8,128)}) custom-call(f32[4,2,32,128]{3,2,1,0:T(8,128)} %copy-done.1, f32[32,128,128]{2,1,0:T(8,128)} %bitcast.5), custom_call_target="tpu_custom_call" | custom-call | tf_op jit(solution)/shard_map/finish/pallas_call | solution.py:301
Async XLA Ops:
  0.6 1.6 %copy-start = (f32[1,32,128,128]{3,2,1,0:T(8,128)S(1)}, f32[1,32,128,128]{3,2,1,0:T(8,128)}, u32[]{:S(2)}) copy-start(f32[1,32,128,128]{3,2,1,0:T(8,128)} %param.5) | copy-start | bytes 6291460
  2.2 0.7 %copy-start.2 = (f32[1,32,128]{2,1,0:T(8,128)S(1)}, f32[1,32,128]{2,1,0:T(8,128)}, u32[]{:S(2)}) copy-start(f32[1,32,128]{2,1,0:T(8,128)} %param.9) | copy-start | bytes 49156
  2.9 0.7 %copy-start.3 = (s32[64]{0:T(128)S(1)}, s32[64]{0:T(128)}, u32[]{:S(2)}) copy-start(s32[64]{0:T(128)} %parents.1) | copy-start | bytes 772
  3.6 0.7 %copy-start.4 = (s32[64]{0:T(128)S(1)}, s32[64]{0:T(128)}, u32[]{:S(2)}) copy-start(s32[64]{0:T(128)} %kinds.1) | copy-start | bytes 772
  4.3 0.7 %copy-start.5 = (s32[64]{0:T(128)S(1)}, s32[64]{0:T(128)}, u32[]{:S(2)}) copy-start(s32[64]{0:T(128)} %param.8) | copy-start | bytes 772
  52.9 0.6 %copy-start.1 = (f32[4,2,32,128]{3,2,1,0:T(8,128)}, f32[4,2,32,128]{3,2,1,0:T(8,128)S(1)}, u32[]{:S(2)}) copy-start(f32[4,2,32,128]{3,2,1,0:T(8,128)S(1)} %sweep.1.final) | copy-start | bytes 393220

commit v2 on v1

v2 whole, which is shorter than its diff:
```python
import jax
import jax.numpy as jnp
from jax import lax
from jax.experimental import pallas as pl
from jax.experimental.pallas import tpu as pltpu
from jax.sharding import PartitionSpec as P

MESH = pl.DeviceIdType.MESH
K = 128
QUARTERS = 4
ROWS = K // QUARTERS
CLIQUES = 64
LEVEL1, LEVEL2 = 5, 21
FIRST = LEVEL1 - 1
SECOND = LEVEL2 - LEVEL1
LEAVES = CLIQUES - LEVEL2
SUB = ROWS // SECOND


def sweep_kernel(
    parents_hbm, kinds_hbm, targets_hbm, pot_hbm, measured_hbm, out, pot,
    parents, kinds, targets, measured,
    partial, partial_in, own_l0, whole_l0, message, message_t, pot_t, tables,
    to_first, to_second, candidates, sub_tables, relay_tables,
    sub_measured, forwarded, relay_measured, to_leaf, from_relay,
    sem_small, sem_pot,
    sem_l0, sem_whole, sem_first, sem_second, sem_rows, sem_relay, sem_forward, sem_measured, sem_leaf,
):
    me = lax.axis_index("wide")
    quarter = lax.axis_index("narrow")
    is_root = me == 0
    is_first = jnp.logical_and(me >= 1, me < LEVEL1)
    is_second = jnp.logical_and(me >= LEVEL1, me < LEVEL2)
    is_leaf = me >= LEVEL2
    is_inner = me < LEVEL2
    peers = QUARTERS - 1

    def peer(step):
        return lax.rem(quarter + step, QUARTERS)

    def rows_of(part):
        return pl.ds(pl.multiple_of(part * ROWS, ROWS), ROWS)

    def repeat(count, function, unroll=1):
        def run(index, carry):
            function(index)
            return carry

        lax.fori_loop(0, count, run, 0, unroll=unroll)

    def send(source, target, sem, device):
        pltpu.make_async_remote_copy(
            src_ref=source, dst_ref=target, send_sem=sem.at[0], recv_sem=sem.at[1],
            device_id=device, device_id_type=MESH,
        ).start()

    def await_bytes(like, sem, which):
        pltpu.make_async_copy(like, like, sem.at[which]).wait()

    small = [
        pltpu.make_async_copy(source, target, sem_small.at[index])
        for index, (source, target) in enumerate(
            ((parents_hbm, parents), (kinds_hbm, kinds), (targets_hbm, targets), (measured_hbm, measured))
        )
    ]

    def pot_copy(step):
        rows = rows_of(peer(step))
        return pltpu.make_async_copy(pot_hbm.at[:, rows], pot.at[:, rows], sem_pot.at[step])

    order = (1, 2, 3, 0)
    for step in order:
        pot_copy(step).start()
    for copy in small:
        copy.start()

    barrier = pltpu.get_barrier_semaphore()

    def greet(wide, narrow):
        pl.semaphore_signal(barrier, inc=1, device_id=(wide, narrow), device_id_type=MESH)

    for step in range(1, QUARTERS):
        greet(me, peer(step))

    @pl.when(is_first)
    def _():
        greet(0, quarter)

    @pl.when(is_second)
    def _():
        def one(index):
            greet(1 + index + (index >= me - 1).astype(jnp.int32), quarter)

        repeat(CLIQUES - 2, one)

    @pl.when(is_leaf)
    def _():
        def one(index):
            greet(LEVEL1 + index // QUARTERS, lax.rem(index, QUARTERS))

        repeat(SECOND * QUARTERS, one)

    def partial_lse(step):
        base = peer(step) * ROWS

        def one(block):
            rows = pl.ds(pl.multiple_of(base + block * 8, 8), 8)
            slab = pot[:, rows, :]
            largest = jnp.max(slab, axis=0)
            partial[rows, :] = largest + jnp.log(jnp.sum(jnp.exp(slab - largest[None]), axis=0))

        pot_copy(step).wait()
        repeat(ROWS // 8, one, unroll=2)

    partial_lse(1)

    @pl.when(is_root)
    def _():
        pl.semaphore_wait(barrier, peers + FIRST)

    @pl.when(is_first)
    def _():
        pl.semaphore_wait(barrier, peers + SECOND)

    @pl.when(is_leaf)
    def _():
        pl.semaphore_wait(barrier, peers + SECOND)

    @pl.when(is_second)
    def _():
        pl.semaphore_wait(barrier, peers + SECOND - 1 + LEAVES * QUARTERS)

    for step in order:
        if step != order[0]:
            partial_lse(step)
        if step:
            send(partial.at[rows_of(peer(step))], partial_in.at[step - 1], sem_l0, (me, peer(step)))

    for copy in small:
        copy.wait()
    for relay in range(SECOND):
        sub_measured[relay] = measured[relay * SUB:(relay + 1) * SUB, :]

    @pl.when(is_root)
    def _():
        send(sub_measured, forwarded, sem_forward, (1, quarter))

    @pl.when(jnp.logical_not(is_root))
    def _():
        def give(relay):
            @pl.when(me != LEVEL1 + relay)
            def _():
                send(sub_measured.at[relay], relay_measured.at[me], sem_measured, (LEVEL1 + relay, quarter))

        repeat(SECOND, give)

    @pl.when(me == 1)
    def _():
        await_bytes(forwarded, sem_forward, 1)

        def give(relay):
            send(forwarded.at[relay], relay_measured.at[0], sem_measured, (LEVEL1 + relay, quarter))

        repeat(SECOND, give)

    @pl.when(is_inner)
    def _():
        def turn(a0):
            pot_t[a0] = pot[a0].T

        repeat(ROWS, turn, unroll=4)

    @pl.when(is_root)
    def _():
        message[...] = jnp.zeros_like(message)

    @pl.when(is_first)
    def _():
        await_bytes(message, sem_first, 1)

    @pl.when(is_second)
    def _():
        await_bytes(candidates, sem_second, 1)
        message[quarter] = candidates[jnp.maximum(parents[me] - 1, 0)]
        for step in range(1, QUARTERS):
            send(message.at[quarter], message.at[quarter], sem_rows, (me, peer(step)))
        await_bytes(message.at[pl.ds(0, QUARTERS - 1)], sem_rows, 1)

    @pl.when(is_inner)
    def _():
        for other in range(QUARTERS):
            message_t[:, other * ROWS:(other + 1) * ROWS] = message[other].T

        def eight(group):
            rows = pl.ds(pl.multiple_of(group * 8, 8), 8)
            for kind in (1, 2):
                tops, totals = [], []
                for step in range(8):
                    a0 = group * 8 + step
                    if kind == 1:
                        belief = (pot[a0].reshape(QUARTERS, ROWS, K) + message[...]).reshape(K, K)
                    else:
                        belief = pot_t[a0] + message_t[...]
                    largest = jnp.max(belief, axis=0, keepdims=True)
                    tops.append(largest)
                    totals.append(jnp.sum(jnp.exp(belief - largest), axis=0, keepdims=True))
                tables[kind, rows, :] = jnp.concatenate(tops, 0) + jnp.log(jnp.concatenate(totals, 0))

        repeat(ROWS // 8, eight)

    await_bytes(partial_in, sem_l0, 1)
    mine = partial[rows_of(quarter), :]
    largest = jnp.maximum(mine, jnp.max(partial_in[...], axis=0))
    summed = jnp.exp(mine - largest) + jnp.sum(jnp.exp(partial_in[...] - largest[None]), axis=0)
    own_l0[...] = largest + jnp.log(summed)

    @pl.when(is_inner)
    def _():
        tables[0] = own_l0[...] + message[quarter]

    @pl.when(is_root)
    def _():
        for child in range(FIRST):
            to_first[child] = tables[kinds[1 + child]]
            for other in range(QUARTERS):
                send(to_first.at[child], message.at[quarter], sem_first, (1 + child, other))

    @pl.when(is_first)
    def _():
        def give(child):
            to_second[child] = tables[kinds[LEVEL1 + child]]
            send(to_second.at[child], candidates.at[me - 1], sem_second, (LEVEL1 + child, quarter))

        repeat(SECOND, give)

    @pl.when(is_second)
    def _():
        slot = me - LEVEL1
        for kind in range(3):
            for relay in range(SECOND):
                sub_tables[relay, kind] = tables[kind, relay * SUB:(relay + 1) * SUB, :]

        def give_tables(relay):
            @pl.when(slot != relay)
            def _():
                send(sub_tables.at[relay], relay_tables.at[slot], sem_relay, (LEVEL1 + relay, quarter))

        repeat(SECOND, give_tables)

    for step in range(1, QUARTERS):
        send(own_l0, whole_l0.at[quarter], sem_whole, (me, peer(step)))
    whole_l0[quarter] = own_l0[...]

    @pl.when(is_second)
    def _():
        slot = me - LEVEL1
        relay_tables[slot] = sub_tables[slot]
        await_bytes(relay_measured.at[pl.ds(0, CLIQUES - 1)], sem_measured, 1)
        relay_measured[me] = sub_measured[slot]
        clique = lax.broadcasted_iota(jnp.int32, (CLIQUES, CLIQUES), 0)
        chosen = (clique == targets[...]).astype(jnp.float32)
        for row in range(SUB):
            to_leaf[:, 1, row, :] = jnp.dot(
                chosen, relay_measured[:, row, :],
                precision=lax.Precision.HIGHEST, preferred_element_type=jnp.float32,
            )
        await_bytes(relay_tables.at[pl.ds(0, SECOND - 1)], sem_relay, 1)
        place = quarter * SECOND + slot

        def give_leaf(leaf):
            child = LEVEL2 + leaf
            to_leaf[child, 0] = relay_tables[jnp.maximum(parents[child] - LEVEL1, 0), kinds[child]]
            for other in range(QUARTERS):
                send(to_leaf.at[child], from_relay.at[place], sem_leaf, (child, other))

        repeat(LEAVES, give_leaf)

    await_bytes(whole_l0.at[pl.ds(0, QUARTERS - 1)], sem_whole, 1)

    @pl.when(is_inner)
    def _():
        out[:, 0] = whole_l0[...] + message[...]
        out[:, 1] = jnp.zeros((QUARTERS, ROWS, K), jnp.float32)

    @pl.when(is_leaf)
    def _():
        await_bytes(from_relay, sem_leaf, 1)
        for other in range(QUARTERS):
            for relay in range(SECOND):
                rows = slice(relay * SUB, (relay + 1) * SUB)
                place = other * SECOND + relay
                out[other, 0, rows, :] = whole_l0[other, rows, :] + from_relay[place, 0]
                out[other, 1, rows, :] = from_relay[place, 1]

    await_bytes(partial_in, sem_l0, 0)
    await_bytes(whole_l0.at[pl.ds(0, QUARTERS - 1)], sem_whole, 0)

    @pl.when(is_root)
    def _():
        await_bytes(sub_measured, sem_forward, 0)
        for _ in range(QUARTERS):
            await_bytes(to_first, sem_first, 0)

    @pl.when(is_first)
    def _():
        await_bytes(to_second, sem_second, 0)

    @pl.when(me == 1)
    def _():
        await_bytes(forwarded, sem_measured, 0)

    @pl.when(is_second)
    def _():
        await_bytes(message.at[pl.ds(0, QUARTERS - 1)], sem_rows, 0)
        await_bytes(relay_tables.at[pl.ds(0, SECOND - 1)], sem_relay, 0)
        await_bytes(relay_measured.at[pl.ds(0, SECOND - 1)], sem_measured, 0)
        for _ in range(QUARTERS):
            await_bytes(to_leaf.at[pl.ds(0, LEAVES)], sem_leaf, 0)

    @pl.when(jnp.logical_or(is_first, is_leaf))
    def _():
        await_bytes(sub_measured, sem_measured, 0)


def sweep(parents, kinds, targets, pot, measured):
    hbm, vmem = pl.BlockSpec(memory_space=pltpu.HBM), pl.BlockSpec(memory_space=pltpu.VMEM)
    f32 = jnp.float32
    scratch = [
        (ROWS, K),
        (K, K), (QUARTERS - 1, ROWS, K), (ROWS, K), (QUARTERS, ROWS, K), (QUARTERS, ROWS, K), (K, K), (ROWS, K, K),
        (3, ROWS, K),
        (FIRST, ROWS, K), (SECOND, ROWS, K), (FIRST, ROWS, K), (SECOND, 3, SUB, K), (SECOND, 3, SUB, K),
        (SECOND, SUB, K), (SECOND, SUB, K), (CLIQUES, SUB, K), (CLIQUES, 2, SUB, K), (CLIQUES, 2, SUB, K),
    ]
    return pl.pallas_call(
        sweep_kernel,
        out_shape=(
            jax.ShapeDtypeStruct((QUARTERS, 2, ROWS, K), f32),
            jax.ShapeDtypeStruct((ROWS, K, K), f32),
        ),
        in_specs=[hbm] * 5,
        out_specs=(vmem, vmem),
        scratch_shapes=[
            pltpu.SMEM((CLIQUES,), jnp.int32), pltpu.SMEM((CLIQUES,), jnp.int32), pltpu.VMEM((1, CLIQUES), jnp.int32),
            *(pltpu.VMEM(shape, f32) for shape in scratch),
            pltpu.SemaphoreType.DMA((4,)), pltpu.SemaphoreType.DMA((QUARTERS,)),
            *[pltpu.SemaphoreType.DMA((2,))] * 9,
        ],
        compiler_params=pltpu.CompilerParams(
            collective_id=0, has_side_effects=True, vmem_limit_bytes=16 * 1024 * 1024
        ),
        name="sweep",
    )(parents, kinds, targets, pot, measured)


BLOCK = 8


def finish_kernel(final, pot, marginal_hbm, updated_hbm, marginal, updated, sem):
    me = lax.axis_index("wide")
    quarter = lax.axis_index("narrow")
    cells = final[:, 0]
    largest = jnp.max(cells)
    weights = jnp.exp(cells - largest)
    scale = jnp.float32(K * K) / jnp.sum(weights)
    whole = weights * scale
    marginal[...] = jnp.exp(final[quarter, 0] - largest) * scale
    copies = [pltpu.make_async_copy(marginal, marginal_hbm, sem.at[0])]
    copies[0].start()
    term = jnp.where(me >= LEVEL2, jnp.float32(0.5) * (whole - final[:, 1]), jnp.float32(0.0)).reshape(K, K)
    for block in range(ROWS // BLOCK):
        rows = slice(block * BLOCK, (block + 1) * BLOCK)
        updated[rows] = pot[rows] - term[None]
        copies.append(pltpu.make_async_copy(updated.at[rows], updated_hbm.at[rows], sem.at[1 + block]))
        copies[-1].start()
    for copy in copies:
        copy.wait()


def finish(final, pot):
    hbm, vmem = pl.BlockSpec(memory_space=pltpu.HBM), pl.BlockSpec(memory_space=pltpu.VMEM)
    shapes = (ROWS, K), (ROWS, K, K)
    return pl.pallas_call(
        finish_kernel,
        out_shape=tuple(jax.ShapeDtypeStruct(shape, jnp.float32) for shape in shapes),
        in_specs=[vmem, vmem],
        out_specs=(hbm, hbm),
        scratch_shapes=[*(pltpu.VMEM(shape, jnp.float32) for shape in shapes), pltpu.SemaphoreType.DMA((1 + ROWS // BLOCK,))],
        compiler_params=pltpu.CompilerParams(vmem_limit_bytes=16 * 1024 * 1024),
        name="finish",
    )(final, pot)


def body(potentials, parents, separator_excluded, measurement_clique, measured):
    parents, separator_excluded, measurement_clique, measured, potentials = (
        pltpu.with_memory_space_constraint(array, pltpu.HBM)
        for array in (parents, separator_excluded, measurement_clique[None], measured[0], potentials[0])
    )
    pot = potentials
    final, pot = sweep(parents, separator_excluded, measurement_clique, pot, measured)
    marginal, updated = finish(final, pot)
    return marginal[None], updated[None]


def solution(mesh):
    return jax.shard_map(
        body,
        mesh=mesh,
        in_specs=(P("wide", "narrow", None, None), P(), P(), P(), P("wide", "narrow", None)),
        out_specs=(P("wide", "narrow", None), P("wide", "narrow", None, None)),
        check_vma=False,
    )
```

time: 58.5 us -> 44 us (0.75); the launches traced: 57.7 us -> 43.9 us
  Pallas kernels: 52.1 us -> 43.2 us
  local copies, waits for them, and re-layouts: 4.91 us -> 0 us
    pallas_call x2, Pallas kernels: 52.1 us -> 43.2 us  [the longest x1 41.5 us: sweep(): pl.pallas_call(sweep_kernel, out_shape=(jax.ShapeDtypeStruct((QUARTERS, 2...]
    unnamed x12 -> x0, local copies, waits for them, and re-layouts: 4.91 us -> none
where the time goes in v2:
time: 44 us; the launch traced here: 43.9 us
  Pallas kernels  43.2 us (98%)
  between operations  0.64 us (1%)
    pallas_call x1, Pallas kernels, sweep(): pl.pallas_call(sweep_kernel, out_shape=(jax.ShapeDtypeStruct((QUARTERS, 2...  41.5 us
    pallas_call x1, Pallas kernels, finish(): pl.pallas_call(finish_kernel, out_shape=tuple((jax.ShapeDtypeStruct(shape...  1.7 us

profile of v2, /device:TPU:7, one launch (start us, length us, event | category | flops | bytes accessed | tf_op | source)
XLA Modules:
  0.0 43.9 jit_solution(7330829134715040483)
XLA Ops:
  0.6 41.5 %sweep.1 = (f32[4,2,32,128]{3,2,1,0:T(8,128)S(1)}, f32[32,128,128]{2,1,0:T(8,128)S(1)}) custom-call(s32[64]{0:T(128)} %parents_hbm.1, s32[64]{0:T(128)} %kinds_hbm.1, s32[1,64]{1,0:T(1,128)} %bitcast.7, f32[32,128,128]{2,1,0:T(8,128)} %bitcast.5, f32[32,128]{1,0:T(8,128)} %bitcast.6), custom_call_target="tpu_custom_call" | custom-call | tf_op jit(solution)/shard_map/sweep/pallas_call | solution.py:335
  42.2 1.7 %finish.1 = (f32[32,128]{1,0:T(8,128)}, f32[32,128,128]{2,1,0:T(8,128)}) custom-call(f32[4,2,32,128]{3,2,1,0:T(8,128)S(1)} %get-tuple-element.6.final, f32[32,128,128]{2,1,0:T(8,128)S(1)} %get-tuple-element.7.pot), custom_call_target="tpu_custom_call" | custom-call | tf_op jit(solution)/shard_map/finish/pallas_call | solution.py:383

commit v3 on v2

--- a/solution.py
+++ b/solution.py
@@ -22,9 +22,9 @@
     parents, kinds, targets, measured,
     partial, partial_in, own_l0, whole_l0, message, message_t, pot_t, tables,
     to_first, to_second, candidates, sub_tables, relay_tables,
-    sub_measured, forwarded, relay_measured, to_leaf, from_relay,
+    sub_measured, forwarded, relay_measured, measured_to_leaf, whole_measured, to_leaf, from_relay,
     sem_small, sem_pot,
-    sem_l0, sem_whole, sem_first, sem_second, sem_rows, sem_relay, sem_forward, sem_measured, sem_leaf,
+    sem_l0, sem_whole, sem_first, sem_second, sem_rows, sem_relay, sem_forward, sem_measured, sem_given, sem_gather, sem_leaf,
 ):
     me = lax.axis_index("wide")
     quarter = lax.axis_index("narrow")
@@ -169,6 +169,25 @@
             pot_t[a0] = pot[a0].T
 
         repeat(ROWS, turn, unroll=4)
+
+    @pl.when(is_second)
+    def _():
+        slot = me - LEVEL1
+        await_bytes(relay_measured.at[pl.ds(0, CLIQUES - 1)], sem_measured, 1)
+        relay_measured[me] = sub_measured[slot]
+        clique = lax.broadcasted_iota(jnp.int32, (CLIQUES, CLIQUES), 0)
+        chosen = (clique == targets[...]).astype(jnp.float32)
+        for row in range(SUB):
+            measured_to_leaf[:, row, :] = jnp.dot(
+                chosen, relay_measured[:, row, :],
+                precision=lax.Precision.HIGHEST, preferred_element_type=jnp.float32,
+            )
+
+        def give(leaf):
+            child = LEVEL2 + leaf
+            send(measured_to_leaf.at[child], whole_measured.at[quarter, slot], sem_given, (child, quarter))
+
+        repeat(LEAVES, give)
 
     @pl.when(is_root)
     def _():
@@ -255,23 +274,14 @@
     def _():
         slot = me - LEVEL1
         relay_tables[slot] = sub_tables[slot]
-        await_bytes(relay_measured.at[pl.ds(0, CLIQUES - 1)], sem_measured, 1)
-        relay_measured[me] = sub_measured[slot]
-        clique = lax.broadcasted_iota(jnp.int32, (CLIQUES, CLIQUES), 0)
-        chosen = (clique == targets[...]).astype(jnp.float32)
-        for row in range(SUB):
-            to_leaf[:, 1, row, :] = jnp.dot(
-                chosen, relay_measured[:, row, :],
-                precision=lax.Precision.HIGHEST, preferred_element_type=jnp.float32,
-            )
         await_bytes(relay_tables.at[pl.ds(0, SECOND - 1)], sem_relay, 1)
         place = quarter * SECOND + slot
 
         def give_leaf(leaf):
             child = LEVEL2 + leaf
-            to_leaf[child, 0] = relay_tables[jnp.maximum(parents[child] - LEVEL1, 0), kinds[child]]
+            to_leaf[leaf] = relay_tables[jnp.maximum(parents[child] - LEVEL1, 0), kinds[child]]
             for other in range(QUARTERS):
-                send(to_leaf.at[child], from_relay.at[place], sem_leaf, (child, other))
+                send(to_leaf.at[leaf], from_relay.at[place], sem_leaf, (child, other))
 
         repeat(LEAVES, give_leaf)
 
@@ -284,13 +294,19 @@
 
     @pl.when(is_leaf)
     def _():
+        await_bytes(whole_measured.at[0], sem_given, 1)
+        for step in range(1, QUARTERS):
+            send(whole_measured.at[quarter], whole_measured.at[quarter], sem_gather, (me, peer(step)))
+        await_bytes(whole_measured.at[pl.ds(0, QUARTERS - 1)], sem_gather, 1)
+        for other in range(QUARTERS):
+            for relay in range(SECOND):
+                out[other, 1, relay * SUB:(relay + 1) * SUB, :] = whole_measured[other, relay]
         await_bytes(from_relay, sem_leaf, 1)
         for other in range(QUARTERS):
             for relay in range(SECOND):
                 rows = slice(relay * SUB, (relay + 1) * SUB)
                 place = other * SECOND + relay
-                out[other, 0, rows, :] = whole_l0[other, rows, :] + from_relay[place, 0]
-                out[other, 1, rows, :] = from_relay[place, 1]
+                out[other, 0, rows, :] = whole_l0[other, rows, :] + from_relay[place]
 
     await_bytes(partial_in, sem_l0, 0)
     await_bytes(whole_l0.at[pl.ds(0, QUARTERS - 1)], sem_whole, 0)
@@ -314,8 +330,13 @@
         await_bytes(message.at[pl.ds(0, QUARTERS - 1)], sem_rows, 0)
         await_bytes(relay_tables.at[pl.ds(0, SECOND - 1)], sem_relay, 0)
         await_bytes(relay_measured.at[pl.ds(0, SECOND - 1)], sem_measured, 0)
+        await_bytes(measured_to_leaf.at[pl.ds(0, LEAVES)], sem_given, 0)
         for _ in range(QUARTERS):
-            await_bytes(to_leaf.at[pl.ds(0, LEAVES)], sem_leaf, 0)
+            await_bytes(to_leaf, sem_leaf, 0)
+
+    @pl.when(is_leaf)
+    def _():
+        await_bytes(whole_measured.at[pl.ds(0, QUARTERS - 1)], sem_gather, 0)
 
     @pl.when(jnp.logical_or(is_first, is_leaf))
     def _():
@@ -330,7 +351,8 @@
         (K, K), (QUARTERS - 1, ROWS, K), (ROWS, K), (QUARTERS, ROWS, K), (QUARTERS, ROWS, K), (K, K), (ROWS, K, K),
         (3, ROWS, K),
         (FIRST, ROWS, K), (SECOND, ROWS, K), (FIRST, ROWS, K), (SECOND, 3, SUB, K), (SECOND, 3, SUB, K),
-        (SECOND, SUB, K), (SECOND, SUB, K), (CLIQUES, SUB, K), (CLIQUES, 2, SUB, K), (CLIQUES, 2, SUB, K),
+        (SECOND, SUB, K), (SECOND, SUB, K), (CLIQUES, SUB, K), (CLIQUES, SUB, K), (QUARTERS, SECOND, SUB, K),
+        (LEAVES, SUB, K), (CLIQUES, SUB, K),
     ]
     return pl.pallas_call(
         sweep_kernel,
@@ -344,7 +366,7 @@
             pltpu.SMEM((CLIQUES,), jnp.int32), pltpu.SMEM((CLIQUES,), jnp.int32), pltpu.VMEM((1, CLIQUES), jnp.int32),
             *(pltpu.VMEM(shape, f32) for shape in scratch),
             pltpu.SemaphoreType.DMA((4,)), pltpu.SemaphoreType.DMA((QUARTERS,)),
-            *[pltpu.SemaphoreType.DMA((2,))] * 9,
+            *[pltpu.SemaphoreType.DMA((2,))] * 11,
         ],
         compiler_params=pltpu.CompilerParams(
             collective_id=0, has_side_effects=True, vmem_limit_bytes=16 * 1024 * 1024

time: 44 us -> 40.8 us (0.927)
  Pallas kernels: 43.2 us -> 40.1 us
    pallas_call x1, Pallas kernels: 41.5 us -> 38.4 us  [sweep(): pl.pallas_call(sweep_kernel, out_shape=(jax.ShapeDtypeStruct((QUARTERS, 2...]
where the time goes in v3:
time: 40.8 us; the launch traced here: 40.7 us
  Pallas kernels  40.1 us (98%)
  between operations  0.64 us (2%)
    pallas_call x1, Pallas kernels, sweep(): pl.pallas_call(sweep_kernel, out_shape=(jax.ShapeDtypeStruct((QUARTERS, 2...  38.4 us
    pallas_call x1, Pallas kernels, finish(): pl.pallas_call(finish_kernel, out_shape=tuple((jax.ShapeDtypeStruct(shape...  1.7 us

profile of v3, /device:TPU:7, one launch (start us, length us, event | category | flops | bytes accessed | tf_op | source)
XLA Modules:
  0.0 40.7 jit_solution(14327180005724691879)
XLA Ops:
  0.6 38.4 %sweep.1 = (f32[4,2,32,128]{3,2,1,0:T(8,128)S(1)}, f32[32,128,128]{2,1,0:T(8,128)S(1)}) custom-call(s32[64]{0:T(128)} %parents_hbm.1, s32[64]{0:T(128)} %kinds_hbm.1, s32[1,64]{1,0:T(1,128)} %bitcast.7, f32[32,128,128]{2,1,0:T(8,128)} %bitcast.5, f32[32,128]{1,0:T(8,128)} %bitcast.6), custom_call_target="tpu_custom_call" | custom-call | tf_op jit(solution)/shard_map/sweep/pallas_call | solution.py:357
  39.0 1.7 %finish.1 = (f32[32,128]{1,0:T(8,128)}, f32[32,128,128]{2,1,0:T(8,128)}) custom-call(f32[4,2,32,128]{3,2,1,0:T(8,128)S(1)} %get-tuple-element.6.final, f32[32,128,128]{2,1,0:T(8,128)S(1)} %get-tuple-element.7.pot), custom_call_target="tpu_custom_call" | custom-call | tf_op jit(solution)/shard_map/finish/pallas_call | solution.py:405

commit v4 on v2

--- a/solution.py
+++ b/solution.py
@@ -14,7 +14,9 @@
 FIRST = LEVEL1 - 1
 SECOND = LEVEL2 - LEVEL1
 LEAVES = CLIQUES - LEVEL2
-SUB = ROWS // SECOND
+RELAYS = 16
+FRONT = 2 * RELAYS
+SUB = ROWS // RELAYS
 
 
 def sweep_kernel(
@@ -22,9 +24,10 @@
     parents, kinds, targets, measured,
     partial, partial_in, own_l0, whole_l0, message, message_t, pot_t, tables,
     to_first, to_second, candidates, sub_tables, relay_tables,
-    sub_measured, forwarded, relay_measured, to_leaf, from_relay,
+    sub_measured, forwarded, relay_measured, measured_to_leaf, whole_measured, to_leaf, from_relay,
     sem_small, sem_pot,
-    sem_l0, sem_whole, sem_first, sem_second, sem_rows, sem_relay, sem_forward, sem_measured, sem_leaf,
+    sem_l0, sem_whole, sem_first, sem_second, sem_rows, sem_relay, sem_forward, sem_measured, sem_given, sem_gather, sem_leaf,
+    sem_near, sem_far,
 ):
     me = lax.axis_index("wide")
     quarter = lax.axis_index("narrow")
@@ -33,6 +36,9 @@
     is_second = jnp.logical_and(me >= LEVEL1, me < LEVEL2)
     is_leaf = me >= LEVEL2
     is_inner = me < LEVEL2
+    odd = lax.rem(me, 2)
+    is_relay = jnp.logical_and(odd == 1, me < FRONT)
+    is_early = me < LEVEL1
     peers = QUARTERS - 1
 
     def peer(step):
@@ -69,6 +75,7 @@
         return pltpu.make_async_copy(pot_hbm.at[:, rows], pot.at[:, rows], sem_pot.at[step])
 
     order = (1, 2, 3, 0)
+    far_first = (2, 1, 3, 0)
     for step in order:
         pot_copy(step).start()
     for copy in small:
@@ -82,23 +89,27 @@
     for step in range(1, QUARTERS):
         greet(me, peer(step))
 
+    @pl.when(is_root)
+    def _():
+        for child in range(1, LEVEL1):
+            greet(child, quarter)
+
     @pl.when(is_first)
     def _():
-        greet(0, quarter)
-
-    @pl.when(is_second)
+        for step in range(FIRST - 1):
+            greet(1 + lax.rem(me + step, FIRST), quarter)
+        repeat(FRONT - LEVEL1, lambda index: greet(LEVEL1 + index, quarter))
+
+    @pl.when(jnp.logical_and(is_first, is_relay))
+    def _():
+        repeat(CLIQUES - FRONT, lambda index: greet(FRONT + index, quarter))
+
+    @pl.when(jnp.logical_and(jnp.logical_not(is_early), is_relay))
     def _():
         def one(index):
-            greet(1 + index + (index >= me - 1).astype(jnp.int32), quarter)
-
-        repeat(CLIQUES - 2, one)
-
-    @pl.when(is_leaf)
-    def _():
-        def one(index):
-            greet(LEVEL1 + index // QUARTERS, lax.rem(index, QUARTERS))
-
-        repeat(SECOND * QUARTERS, one)
+            greet(LEVEL1 + index + (index >= me - LEVEL1).astype(jnp.int32), quarter)
+
+        repeat(CLIQUES - LEVEL1 - 1, one)
 
     def partial_lse(step):
         base = peer(step) * ROWS
@@ -116,19 +127,22 @@
 
     @pl.when(is_root)
     def _():
+        pl.semaphore_wait(barrier, peers)
+
+    @pl.when(is_first)
+    def _():
         pl.semaphore_wait(barrier, peers + FIRST)
-
-    @pl.when(is_first)
-    def _():
-        pl.semaphore_wait(barrier, peers + SECOND)
-
-    @pl.when(is_leaf)
-    def _():
-        pl.semaphore_wait(barrier, peers + SECOND)
-
-    @pl.when(is_second)
-    def _():
-        pl.semaphore_wait(barrier, peers + SECOND - 1 + LEAVES * QUARTERS)
+        pl.semaphore_signal(sem_near, inc=1, device_id=(0, quarter), device_id_type=MESH)
+
+    @pl.when(jnp.logical_and(jnp.logical_not(is_early), me < FRONT))
+    def _():
+        pl.semaphore_wait(barrier, peers + RELAYS - odd + 2)
+        for child in range(1, LEVEL1):
+            pl.semaphore_signal(sem_far, inc=1, device_id=(child, quarter), device_id_type=MESH)
+
+    @pl.when(me >= FRONT)
+    def _():
+        pl.semaphore_wait(barrier, peers + RELAYS)
 
     for step in order:
         if step != order[0]:
@@ -138,30 +152,17 @@
 
     for copy in small:
         copy.wait()
-    for relay in range(SECOND):
+    for relay in range(RELAYS):
         sub_measured[relay] = measured[relay * SUB:(relay + 1) * SUB, :]
 
-    @pl.when(is_root)
-    def _():
-        send(sub_measured, forwarded, sem_forward, (1, quarter))
-
-    @pl.when(jnp.logical_not(is_root))
-    def _():
-        def give(relay):
-            @pl.when(me != LEVEL1 + relay)
-            def _():
-                send(sub_measured.at[relay], relay_measured.at[me], sem_measured, (LEVEL1 + relay, quarter))
-
-        repeat(SECOND, give)
-
-    @pl.when(me == 1)
-    def _():
-        await_bytes(forwarded, sem_forward, 1)
-
-        def give(relay):
-            send(forwarded.at[relay], relay_measured.at[0], sem_measured, (LEVEL1 + relay, quarter))
-
-        repeat(SECOND, give)
+    def give_measured(relay):
+        @pl.when(me != 2 * relay + 1)
+        def _():
+            send(sub_measured.at[relay], relay_measured.at[me], sem_measured, (2 * relay + 1, quarter))
+
+    @pl.when(jnp.logical_not(is_early))
+    def _():
+        repeat(RELAYS, give_measured)
 
     @pl.when(is_inner)
     def _():
@@ -220,60 +221,122 @@
 
     @pl.when(is_root)
     def _():
-        for child in range(FIRST):
+        pl.semaphore_wait(sem_near, FIRST)
+        for child in reversed(range(FIRST)):
             to_first[child] = tables[kinds[1 + child]]
-            for other in range(QUARTERS):
-                send(to_first.at[child], message.at[quarter], sem_first, (1 + child, other))
+            for step in far_first:
+                send(to_first.at[child], message.at[quarter], sem_first, (1 + child, peer(step)))
+        send(sub_measured, forwarded, sem_forward, (1, quarter))
 
     @pl.when(is_first)
     def _():
-        def give(child):
+        pl.semaphore_wait(sem_far, FRONT - LEVEL1)
+
+        def give(index):
+            child = lax.rem(index + 3, SECOND)
             to_second[child] = tables[kinds[LEVEL1 + child]]
             send(to_second.at[child], candidates.at[me - 1], sem_second, (LEVEL1 + child, quarter))
 
         repeat(SECOND, give)
+        repeat(RELAYS, give_measured)
+
+    @pl.when(me == 1)
+    def _():
+        await_bytes(forwarded, sem_forward, 1)
+
+        def give(index):
+            relay = 1 + index
+            send(forwarded.at[relay], relay_measured.at[0], sem_measured, (2 * relay + 1, quarter))
+
+        repeat(RELAYS - 1, give)
+        relay_measured[0] = forwarded[0]
 
     @pl.when(is_second)
     def _():
         slot = me - LEVEL1
         for kind in range(3):
-            for relay in range(SECOND):
+            for relay in range(RELAYS):
                 sub_tables[relay, kind] = tables[kind, relay * SUB:(relay + 1) * SUB, :]
 
         def give_tables(relay):
-            @pl.when(slot != relay)
+            @pl.when(me != 2 * relay + 1)
             def _():
-                send(sub_tables.at[relay], relay_tables.at[slot], sem_relay, (LEVEL1 + relay, quarter))
-
-        repeat(SECOND, give_tables)
+                send(sub_tables.at[relay], relay_tables.at[slot], sem_relay, (2 * relay + 1, quarter))
+
+        repeat(RELAYS, give_tables)
 
     for step in range(1, QUARTERS):
         send(own_l0, whole_l0.at[quarter], sem_whole, (me, peer(step)))
     whole_l0[quarter] = own_l0[...]
 
-    @pl.when(is_second)
-    def _():
-        slot = me - LEVEL1
-        relay_tables[slot] = sub_tables[slot]
+    relay_slot = me // 2
+
+    @pl.when(me == 1)
+    def _():
+        await_bytes(relay_measured.at[pl.ds(0, CLIQUES - 2)], sem_measured, 1)
+
+    @pl.when(jnp.logical_and(is_relay, me != 1))
+    def _():
         await_bytes(relay_measured.at[pl.ds(0, CLIQUES - 1)], sem_measured, 1)
-        relay_measured[me] = sub_measured[slot]
+
+    @pl.when(is_relay)
+    def _():
+        relay_measured[me] = sub_measured[relay_slot]
         clique = lax.broadcasted_iota(jnp.int32, (CLIQUES, CLIQUES), 0)
         chosen = (clique == targets[...]).astype(jnp.float32)
         for row in range(SUB):
-            to_leaf[:, 1, row, :] = jnp.dot(
+            measured_to_leaf[:, row, :] = jnp.dot(
                 chosen, relay_measured[:, row, :],
                 precision=lax.Precision.HIGHEST, preferred_element_type=jnp.float32,
             )
+
+        def give(leaf):
+            child = LEVEL2 + leaf
+
+            @pl.when(child != me)
+            def _():
+                send(measured_to_leaf.at[child], whole_measured.at[quarter, relay_slot], sem_given, (child, quarter))
+
+        repeat(LEAVES, give)
+
+    @pl.when(jnp.logical_and(is_relay, is_second))
+    def _():
+        relay_tables[me - LEVEL1] = sub_tables[relay_slot]
         await_bytes(relay_tables.at[pl.ds(0, SECOND - 1)], sem_relay, 1)
-        place = quarter * SECOND + slot
-
-        def give_leaf(leaf):
+
+    @pl.when(jnp.logical_and(is_relay, jnp.logical_not(is_second)))
+    def _():
+        await_bytes(relay_tables, sem_relay, 1)
+
+    @pl.when(is_relay)
+    def _():
+        place = quarter * RELAYS + relay_slot
+
+        def give_leaf(index):
+            leaf = lax.rem(index * (LEAVES // 2), LEAVES)
             child = LEVEL2 + leaf
-            to_leaf[child, 0] = relay_tables[jnp.maximum(parents[child] - LEVEL1, 0), kinds[child]]
-            for other in range(QUARTERS):
-                send(to_leaf.at[child], from_relay.at[place], sem_leaf, (child, other))
+            to_leaf[leaf] = relay_tables[jnp.maximum(parents[child] - LEVEL1, 0), kinds[child]]
+            for step in far_first[:-1]:
+                send(to_leaf.at[leaf], from_relay.at[place], sem_leaf, (child, peer(step)))
+
+            @pl.when(child != me)
+            def _():
+                send(to_leaf.at[leaf], from_relay.at[place], sem_leaf, (child, quarter))
 
         repeat(LEAVES, give_leaf)
+
+    is_both = jnp.logical_and(is_relay, is_leaf)
+    is_plain_leaf = jnp.logical_and(is_leaf, jnp.logical_not(is_relay))
+
+    @pl.when(is_both)
+    def _():
+        whole_measured[quarter, relay_slot] = measured_to_leaf[me]
+        from_relay[quarter * RELAYS + relay_slot] = to_leaf[me - LEVEL2]
+        await_bytes(whole_measured.at[0, pl.ds(0, RELAYS - 1)], sem_given, 1)
+
+    @pl.when(is_plain_leaf)
+    def _():
+        await_bytes(whole_measured.at[0], sem_given, 1)
 
     await_bytes(whole_l0.at[pl.ds(0, QUARTERS - 1)], sem_whole, 1)
 
@@ -284,13 +347,27 @@
 
     @pl.when(is_leaf)
     def _():
+        for step in range(1, QUARTERS):
+            send(whole_measured.at[quarter], whole_measured.at[quarter], sem_gather, (me, peer(step)))
+        await_bytes(whole_measured.at[pl.ds(0, QUARTERS - 1)], sem_gather, 1)
+        for other in range(QUARTERS):
+            for relay in range(RELAYS):
+                out[other, 1, relay * SUB:(relay + 1) * SUB, :] = whole_measured[other, relay]
+
+    @pl.when(is_both)
+    def _():
+        await_bytes(from_relay.at[pl.ds(0, CLIQUES - 1)], sem_leaf, 1)
+
+    @pl.when(is_plain_leaf)
+    def _():
         await_bytes(from_relay, sem_leaf, 1)
+
+    @pl.when(is_leaf)
+    def _():
         for other in range(QUARTERS):
-            for relay in range(SECOND):
+            for relay in range(RELAYS):
                 rows = slice(relay * SUB, (relay + 1) * SUB)
-                place = other * SECOND + relay
-                out[other, 0, rows, :] = whole_l0[other, rows, :] + from_relay[place, 0]
-                out[other, 1, rows, :] = from_relay[place, 1]
+                out[other, 0, rows, :] = whole_l0[other, rows, :] + from_relay[other * RELAYS + relay]
 
     await_bytes(partial_in, sem_l0, 0)
     await_bytes(whole_l0.at[pl.ds(0, QUARTERS - 1)], sem_whole, 0)
@@ -307,17 +384,41 @@
 
     @pl.when(me == 1)
     def _():
-        await_bytes(forwarded, sem_measured, 0)
+        await_bytes(forwarded.at[pl.ds(0, RELAYS - 1)], sem_measured, 0)
 
     @pl.when(is_second)
     def _():
         await_bytes(message.at[pl.ds(0, QUARTERS - 1)], sem_rows, 0)
-        await_bytes(relay_tables.at[pl.ds(0, SECOND - 1)], sem_relay, 0)
-        await_bytes(relay_measured.at[pl.ds(0, SECOND - 1)], sem_measured, 0)
-        for _ in range(QUARTERS):
-            await_bytes(to_leaf.at[pl.ds(0, LEAVES)], sem_leaf, 0)
-
-    @pl.when(jnp.logical_or(is_first, is_leaf))
+
+    @pl.when(jnp.logical_and(is_second, is_relay))
+    def _():
+        await_bytes(sub_tables.at[pl.ds(0, RELAYS - 1)], sem_relay, 0)
+
+    @pl.when(jnp.logical_and(is_second, jnp.logical_not(is_relay)))
+    def _():
+        await_bytes(sub_tables, sem_relay, 0)
+
+    @pl.when(is_relay)
+    def _():
+        await_bytes(sub_measured.at[pl.ds(0, RELAYS - 1)], sem_measured, 0)
+        for _ in range(QUARTERS - 1):
+            await_bytes(to_leaf, sem_leaf, 0)
+
+    @pl.when(is_both)
+    def _():
+        await_bytes(measured_to_leaf.at[pl.ds(0, LEAVES - 1)], sem_given, 0)
+        await_bytes(to_leaf.at[pl.ds(0, LEAVES - 1)], sem_leaf, 0)
+
+    @pl.when(jnp.logical_and(is_relay, is_inner))
+    def _():
+        await_bytes(measured_to_leaf.at[pl.ds(0, LEAVES)], sem_given, 0)
+        await_bytes(to_leaf, sem_leaf, 0)
+
+    @pl.when(is_leaf)
+    def _():
+        await_bytes(whole_measured.at[pl.ds(0, QUARTERS - 1)], sem_gather, 0)
+
+    @pl.when(jnp.logical_not(jnp.logical_or(is_root, is_relay)))
     def _():
         await_bytes(sub_measured, sem_measured, 0)
 
@@ -329,8 +430,9 @@
         (ROWS, K),
         (K, K), (QUARTERS - 1, ROWS, K), (ROWS, K), (QUARTERS, ROWS, K), (QUARTERS, ROWS, K), (K, K), (ROWS, K, K),
         (3, ROWS, K),
-        (FIRST, ROWS, K), (SECOND, ROWS, K), (FIRST, ROWS, K), (SECOND, 3, SUB, K), (SECOND, 3, SUB, K),
-        (SECOND, SUB, K), (SECOND, SUB, K), (CLIQUES, SUB, K), (CLIQUES, 2, SUB, K), (CLIQUES, 2, SUB, K),
+        (FIRST, ROWS, K), (SECOND, ROWS, K), (FIRST, ROWS, K), (RELAYS, 3, SUB, K), (SECOND, 3, SUB, K),
+        (RELAYS, SUB, K), (RELAYS, SUB, K), (CLIQUES, SUB, K), (CLIQUES, SUB, K), (QUARTERS, RELAYS, SUB, K),
+        (LEAVES, SUB, K), (QUARTERS * RELAYS, SUB, K),
     ]
     return pl.pallas_call(
         sweep_kernel,
@@ -344,7 +446,8 @@
             pltpu.SMEM((CLIQUES,), jnp.int32), pltpu.SMEM((CLIQUES,), jnp.int32), pltpu.VMEM((1, CLIQUES), jnp.int32),
             *(pltpu.VMEM(shape, f32) for shape in scratch),
             pltpu.SemaphoreType.DMA((4,)), pltpu.SemaphoreType.DMA((QUARTERS,)),
-            *[pltpu.SemaphoreType.DMA((2,))] * 9,
+            *[pltpu.SemaphoreType.DMA((2,))] * 11,
+            pltpu.SemaphoreType.REGULAR, pltpu.SemaphoreType.REGULAR,
         ],
         compiler_params=pltpu.CompilerParams(
             collective_id=0, has_side_effects=True, vmem_limit_bytes=16 * 1024 * 1024

time: 44 us -> 38.3 us (0.87)
  Pallas kernels: 43.2 us -> 37.5 us
    pallas_call x1, Pallas kernels: 41.5 us -> 35.8 us  [sweep(): pl.pallas_call(sweep_kernel, out_shape=(jax.ShapeDtypeStruct((QUARTERS, 2...]
where the time goes in v4:
time: 38.3 us; the launch traced here: 38.2 us
  Pallas kernels  37.5 us (98%)
  between operations  0.64 us (2%)
    pallas_call x1, Pallas kernels, sweep(): pl.pallas_call(sweep_kernel, out_shape=(jax.ShapeDtypeStruct((QUARTERS, 2...  35.8 us
    pallas_call x1, Pallas kernels, finish(): pl.pallas_call(finish_kernel, out_shape=tuple((jax.ShapeDtypeStruct(shape...  1.7 us

profile of v4, /device:TPU:7, one launch (start us, length us, event | category | flops | bytes accessed | tf_op | source)
XLA Modules:
  0.0 38.2 jit_solution(15750028540189470005)
XLA Ops:
  0.6 35.8 %sweep.1 = (f32[4,2,32,128]{3,2,1,0:T(8,128)S(1)}, f32[32,128,128]{2,1,0:T(8,128)S(1)}) custom-call(s32[64]{0:T(128)} %parents_hbm.1, s32[64]{0:T(128)} %kinds_hbm.1, s32[1,64]{1,0:T(1,128)} %bitcast.7, f32[32,128,128]{2,1,0:T(8,128)} %bitcast.5, f32[32,128]{1,0:T(8,128)} %bitcast.6), custom_call_target="tpu_custom_call" | custom-call | tf_op jit(solution)/shard_map/sweep/pallas_call | solution.py:437
  36.5 1.7 %finish.1 = (f32[32,128]{1,0:T(8,128)}, f32[32,128,128]{2,1,0:T(8,128)}) custom-call(f32[4,2,32,128]{3,2,1,0:T(8,128)S(1)} %get-tuple-element.6.final, f32[32,128,128]{2,1,0:T(8,128)S(1)} %get-tuple-element.7.pot), custom_call_target="tpu_custom_call" | custom-call | tf_op jit(solution)/shard_map/finish/pallas_call | solution.py:486

commit v5 on v4

--- a/solution.py
+++ b/solution.py
@@ -17,6 +17,7 @@
 RELAYS = 16
 FRONT = 2 * RELAYS
 SUB = ROWS // RELAYS
+CHIPS, PLANES = 8, 3
 
 
 def sweep_kernel(
@@ -121,7 +122,7 @@
             partial[rows, :] = largest + jnp.log(jnp.sum(jnp.exp(slab - largest[None]), axis=0))
 
         pot_copy(step).wait()
-        repeat(ROWS // 8, one, unroll=2)
+        repeat(ROWS // 8, one, unroll=4)
 
     partial_lse(1)
 
@@ -171,9 +172,26 @@
 
         repeat(ROWS, turn, unroll=4)
 
+    def gather_l0():
+        await_bytes(partial_in, sem_l0, 1)
+        mine = partial[rows_of(quarter), :]
+        largest = jnp.maximum(mine, jnp.max(partial_in[...], axis=0))
+        summed = jnp.exp(mine - largest) + jnp.sum(jnp.exp(partial_in[...] - largest[None]), axis=0)
+        own_l0[...] = largest + jnp.log(summed)
+
+    def share_l0():
+        for step in range(1, QUARTERS):
+            send(own_l0, whole_l0.at[quarter], sem_whole, (me, peer(step)))
+        whole_l0[quarter] = own_l0[...]
+
     @pl.when(is_root)
     def _():
         message[...] = jnp.zeros_like(message)
+
+    @pl.when(jnp.logical_not(is_root))
+    def _():
+        gather_l0()
+        share_l0()
 
     @pl.when(is_first)
     def _():
@@ -207,13 +225,11 @@
                     totals.append(jnp.sum(jnp.exp(belief - largest), axis=0, keepdims=True))
                 tables[kind, rows, :] = jnp.concatenate(tops, 0) + jnp.log(jnp.concatenate(totals, 0))
 
-        repeat(ROWS // 8, eight)
-
-    await_bytes(partial_in, sem_l0, 1)
-    mine = partial[rows_of(quarter), :]
-    largest = jnp.maximum(mine, jnp.max(partial_in[...], axis=0))
-    summed = jnp.exp(mine - largest) + jnp.sum(jnp.exp(partial_in[...] - largest[None]), axis=0)
-    own_l0[...] = largest + jnp.log(summed)
+        repeat(ROWS // 8, eight, unroll=2)
+
+    @pl.when(is_root)
+    def _():
+        gather_l0()
 
     @pl.when(is_inner)
     def _():
@@ -265,9 +281,9 @@
 
         repeat(RELAYS, give_tables)
 
-    for step in range(1, QUARTERS):
-        send(own_l0, whole_l0.at[quarter], sem_whole, (me, peer(step)))
-    whole_l0[quarter] = own_l0[...]
+    @pl.when(is_root)
+    def _():
+        share_l0()
 
     relay_slot = me // 2
 
@@ -313,17 +329,21 @@
         place = quarter * RELAYS + relay_slot
 
         def give_leaf(index):
-            leaf = lax.rem(index * (LEAVES // 2), LEAVES)
-            child = LEVEL2 + leaf
-            to_leaf[leaf] = relay_tables[jnp.maximum(parents[child] - LEVEL1, 0), kinds[child]]
-            for step in far_first[:-1]:
-                send(to_leaf.at[leaf], from_relay.at[place], sem_leaf, (child, peer(step)))
-
-            @pl.when(child != me)
+            plane = lax.rem(index, PLANES * 2)
+            child = 2 * (index // (PLANES * 2)) + 2 * CHIPS * (PLANES - plane // 2) + lax.rem(index, 2)
+            leaf = jnp.maximum(child - LEVEL2, 0)
+
+            @pl.when(child >= LEVEL2)
             def _():
-                send(to_leaf.at[leaf], from_relay.at[place], sem_leaf, (child, quarter))
-
-        repeat(LEAVES, give_leaf)
+                to_leaf[leaf] = relay_tables[jnp.maximum(parents[child] - LEVEL1, 0), kinds[child]]
+                for step in far_first[:-1]:
+                    send(to_leaf.at[leaf], from_relay.at[place], sem_leaf, (child, peer(step)))
+
+                @pl.when(child != me)
+                def _():
+                    send(to_leaf.at[leaf], from_relay.at[place], sem_leaf, (child, quarter))
+
+        repeat(PLANES * CHIPS * 2, give_leaf)
 
     is_both = jnp.logical_and(is_relay, is_leaf)
     is_plain_leaf = jnp.logical_and(is_leaf, jnp.logical_not(is_relay))

time: 38.3 us -> 36.9 us (0.963)
  Pallas kernels: 37.5 us -> 36.1 us
    pallas_call x1, Pallas kernels: 35.8 us -> 34.4 us  [sweep(): pl.pallas_call(sweep_kernel, out_shape=(jax.ShapeDtypeStruct((QUARTERS, 2...]
where the time goes in v5:
time: 36.9 us; the launch traced here: 36.8 us
  Pallas kernels  36.1 us (98%)
  between operations  0.64 us (2%)
    pallas_call x1, Pallas kernels, sweep(): pl.pallas_call(sweep_kernel, out_shape=(jax.ShapeDtypeStruct((QUARTERS, 2...  34.4 us
    pallas_call x1, Pallas kernels, finish(): pl.pallas_call(finish_kernel, out_shape=tuple((jax.ShapeDtypeStruct(shape...  1.7 us

profile of v5, /device:TPU:7, one launch (start us, length us, event | category | flops | bytes accessed | tf_op | source)
XLA Modules:
  0.0 36.8 jit_solution(14154981683895476077)
XLA Ops:
  0.6 34.4 %sweep.1 = (f32[4,2,32,128]{3,2,1,0:T(8,128)S(1)}, f32[32,128,128]{2,1,0:T(8,128)S(1)}) custom-call(s32[64]{0:T(128)} %parents_hbm.1, s32[64]{0:T(128)} %kinds_hbm.1, s32[1,64]{1,0:T(1,128)} %bitcast.7, f32[32,128,128]{2,1,0:T(8,128)} %bitcast.5, f32[32,128]{1,0:T(8,128)} %bitcast.6), custom_call_target="tpu_custom_call" | custom-call | tf_op jit(solution)/shard_map/sweep/pallas_call | solution.py:457
  35.1 1.7 %finish.1 = (f32[32,128]{1,0:T(8,128)}, f32[32,128,128]{2,1,0:T(8,128)}) custom-call(f32[4,2,32,128]{3,2,1,0:T(8,128)S(1)} %get-tuple-element.6.final, f32[32,128,128]{2,1,0:T(8,128)S(1)} %get-tuple-element.7.pot), custom_call_target="tpu_custom_call" | custom-call | tf_op jit(solution)/shard_map/finish/pallas_call | solution.py:506

commit v6 on v5

--- a/solution.py
+++ b/solution.py
@@ -1,3 +1,5 @@
+import functools
+
 import jax
 import jax.numpy as jnp
 from jax import lax
@@ -15,9 +17,14 @@
 SECOND = LEVEL2 - LEVEL1
 LEAVES = CLIQUES - LEVEL2
 RELAYS = 16
-FRONT = 2 * RELAYS
 SUB = ROWS // RELAYS
 CHIPS, PLANES = 8, 3
+
+
+FARTHEST = (5, 7, 6, 8, 11, 3, 9, 12, 4, 10, 13, 1, 14, 2, 15, 0)
+
+
+SERVE = (0, 1, 2, 6, 5, 3, 7, 4)
 
 
 def sweep_kernel(
@@ -38,12 +45,15 @@
     is_leaf = me >= LEVEL2
     is_inner = me < LEVEL2
     odd = lax.rem(me, 2)
-    is_relay = jnp.logical_and(odd == 1, me < FRONT)
+    is_relay = jnp.logical_and(odd == 1, lax.rem(me, 2 * CHIPS) < CHIPS)
     is_early = me < LEVEL1
     peers = QUARTERS - 1
 
     def peer(step):
         return lax.rem(quarter + step, QUARTERS)
+
+    def relay_device(relay):
+        return 2 * CHIPS * (relay // (CHIPS // 2)) + 2 * lax.rem(relay, CHIPS // 2) + 1
 
     def rows_of(part):
         return pl.ds(pl.multiple_of(part * ROWS, ROWS), ROWS)
@@ -75,8 +85,8 @@
         rows = rows_of(peer(step))
         return pltpu.make_async_copy(pot_hbm.at[:, rows], pot.at[:, rows], sem_pot.at[step])
 
-    order = (1, 2, 3, 0)
     far_first = (2, 1, 3, 0)
+    order = far_first
     for step in order:
         pot_copy(step).start()
     for copy in small:
@@ -99,11 +109,7 @@
     def _():
         for step in range(FIRST - 1):
             greet(1 + lax.rem(me + step, FIRST), quarter)
-        repeat(FRONT - LEVEL1, lambda index: greet(LEVEL1 + index, quarter))
-
-    @pl.when(jnp.logical_and(is_first, is_relay))
-    def _():
-        repeat(CLIQUES - FRONT, lambda index: greet(FRONT + index, quarter))
+        repeat(CLIQUES - LEVEL1, lambda index: greet(LEVEL1 + index, quarter))
 
     @pl.when(jnp.logical_and(jnp.logical_not(is_early), is_relay))
     def _():
@@ -124,7 +130,7 @@
         pot_copy(step).wait()
         repeat(ROWS // 8, one, unroll=4)
 
-    partial_lse(1)
+    partial_lse(order[0])
 
     @pl.when(is_root)
     def _():
@@ -135,15 +141,14 @@
         pl.semaphore_wait(barrier, peers + FIRST)
         pl.semaphore_signal(sem_near, inc=1, device_id=(0, quarter), device_id_type=MESH)
 
-    @pl.when(jnp.logical_and(jnp.logical_not(is_early), me < FRONT))
-    def _():
-        pl.semaphore_wait(barrier, peers + RELAYS - odd + 2)
+    @pl.when(jnp.logical_not(is_early))
+    def _():
+        pl.semaphore_wait(barrier, peers + RELAYS - is_relay.astype(jnp.int32) + 2)
+
+    @pl.when(jnp.logical_or(is_second, jnp.logical_and(is_relay, is_leaf)))
+    def _():
         for child in range(1, LEVEL1):
             pl.semaphore_signal(sem_far, inc=1, device_id=(child, quarter), device_id_type=MESH)
-
-    @pl.when(me >= FRONT)
-    def _():
-        pl.semaphore_wait(barrier, peers + RELAYS)
 
     for step in order:
         if step != order[0]:
@@ -157,9 +162,9 @@
         sub_measured[relay] = measured[relay * SUB:(relay + 1) * SUB, :]
 
     def give_measured(relay):
-        @pl.when(me != 2 * relay + 1)
+        @pl.when(me != relay_device(relay))
         def _():
-            send(sub_measured.at[relay], relay_measured.at[me], sem_measured, (2 * relay + 1, quarter))
+            send(sub_measured.at[relay], relay_measured.at[me], sem_measured, (relay_device(relay), quarter))
 
     @pl.when(jnp.logical_not(is_early))
     def _():
@@ -201,7 +206,7 @@
     def _():
         await_bytes(candidates, sem_second, 1)
         message[quarter] = candidates[jnp.maximum(parents[me] - 1, 0)]
-        for step in range(1, QUARTERS):
+        for step in far_first[:-1]:
             send(message.at[quarter], message.at[quarter], sem_rows, (me, peer(step)))
         await_bytes(message.at[pl.ds(0, QUARTERS - 1)], sem_rows, 1)
 
@@ -246,14 +251,12 @@
 
     @pl.when(is_first)
     def _():
-        pl.semaphore_wait(sem_far, FRONT - LEVEL1)
-
-        def give(index):
-            child = lax.rem(index + 3, SECOND)
+        pl.semaphore_wait(sem_far, SECOND + 10)
+
+        for child in FARTHEST:
             to_second[child] = tables[kinds[LEVEL1 + child]]
             send(to_second.at[child], candidates.at[me - 1], sem_second, (LEVEL1 + child, quarter))
 
-        repeat(SECOND, give)
         repeat(RELAYS, give_measured)
 
     @pl.when(me == 1)
@@ -262,7 +265,7 @@
 
         def give(index):
             relay = 1 + index
-            send(forwarded.at[relay], relay_measured.at[0], sem_measured, (2 * relay + 1, quarter))
+            send(forwarded.at[relay], relay_measured.at[0], sem_measured, (relay_device(relay), quarter))
 
         repeat(RELAYS - 1, give)
         relay_measured[0] = forwarded[0]
@@ -275,9 +278,9 @@
                 sub_tables[relay, kind] = tables[kind, relay * SUB:(relay + 1) * SUB, :]
 
         def give_tables(relay):
-            @pl.when(me != 2 * relay + 1)
+            @pl.when(me != relay_device(relay))
             def _():
-                send(sub_tables.at[relay], relay_tables.at[slot], sem_relay, (2 * relay + 1, quarter))
+                send(sub_tables.at[relay], relay_tables.at[slot], sem_relay, (relay_device(relay), quarter))
 
         repeat(RELAYS, give_tables)
 
@@ -285,7 +288,7 @@
     def _():
         share_l0()
 
-    relay_slot = me // 2
+    relay_slot = (CHIPS // 2) * (me // (2 * CHIPS)) + lax.rem(me, 2 * CHIPS) // 2
 
     @pl.when(me == 1)
     def _():
@@ -328,9 +331,8 @@
     def _():
         place = quarter * RELAYS + relay_slot
 
-        def give_leaf(index):
-            plane = lax.rem(index, PLANES * 2)
-            child = 2 * (index // (PLANES * 2)) + 2 * CHIPS * (PLANES - plane // 2) + lax.rem(index, 2)
+        def give_leaf(chip, plane):
+            child = 2 * chip + 2 * CHIPS * (PLANES - plane // 2) + lax.rem(plane, 2)
             leaf = jnp.maximum(child - LEVEL2, 0)
 
             @pl.when(child >= LEVEL2)
@@ -343,7 +345,8 @@
                 def _():
                     send(to_leaf.at[leaf], from_relay.at[place], sem_leaf, (child, quarter))
 
-        repeat(PLANES * CHIPS * 2, give_leaf)
+        for chip in SERVE:
+            repeat(PLANES * 2, functools.partial(give_leaf, chip))
 
     is_both = jnp.logical_and(is_relay, is_leaf)
     is_plain_leaf = jnp.logical_and(is_leaf, jnp.logical_not(is_relay))

time: 36.9 us -> 36.3 us (0.984)
  Pallas kernels: 36.1 us -> 35.5 us
    pallas_call x1, Pallas kernels: 34.4 us -> 33.8 us  [sweep(): pl.pallas_call(sweep_kernel, out_shape=(jax.ShapeDtypeStruct((QUARTERS, 2...]
where the time goes in v6:
time: 36.3 us; the launch traced here: 36.2 us
  Pallas kernels  35.5 us (98%)
  between operations  0.64 us (2%)
    pallas_call x1, Pallas kernels, sweep(): pl.pallas_call(sweep_kernel, out_shape=(jax.ShapeDtypeStruct((QUARTERS, 2...  33.8 us
    pallas_call x1, Pallas kernels, finish(): pl.pallas_call(finish_kernel, out_shape=tuple((jax.ShapeDtypeStruct(shape...  1.7 us

profile of v6, /device:TPU:7, one launch (start us, length us, event | category | flops | bytes accessed | tf_op | source)
XLA Modules:
  0.0 36.2 jit_solution(5957957997099392341)
XLA Ops:
  0.6 33.8 %sweep.1 = (f32[4,2,32,128]{3,2,1,0:T(8,128)S(1)}, f32[32,128,128]{2,1,0:T(8,128)S(1)}) custom-call(s32[64]{0:T(128)} %parents_hbm.1, s32[64]{0:T(128)} %kinds_hbm.1, s32[1,64]{1,0:T(1,128)} %bitcast.7, f32[32,128,128]{2,1,0:T(8,128)} %bitcast.5, f32[32,128]{1,0:T(8,128)} %bitcast.6), custom_call_target="tpu_custom_call" | custom-call | tf_op jit(solution)/shard_map/sweep/pallas_call | solution.py:460
  34.5 1.7 %finish.1 = (f32[32,128]{1,0:T(8,128)}, f32[32,128,128]{2,1,0:T(8,128)}) custom-call(f32[4,2,32,128]{3,2,1,0:T(8,128)S(1)} %get-tuple-element.6.final, f32[32,128,128]{2,1,0:T(8,128)S(1)} %get-tuple-element.7.pot), custom_call_target="tpu_custom_call" | custom-call | tf_op jit(solution)/shard_map/finish/pallas_call | solution.py:509

commit v7 on v6

--- a/solution.py
+++ b/solution.py
@@ -24,7 +24,7 @@
 FARTHEST = (5, 7, 6, 8, 11, 3, 9, 12, 4, 10, 13, 1, 14, 2, 15, 0)
 
 
-SERVE = (0, 1, 2, 6, 5, 3, 7, 4)
+SERVE = (0, 1, 2, 3, 6, 5, 4, 7)
 
 
 def sweep_kernel(

time: 36.3 us -> 36.3 us (level)
  no operation moved by 1% of the time
where the time goes in v7:
time: 36.3 us; the launch traced here: 36.2 us
  Pallas kernels  35.5 us (98%)
  between operations  0.64 us (2%)
    pallas_call x1, Pallas kernels, sweep(): pl.pallas_call(sweep_kernel, out_shape=(jax.ShapeDtypeStruct((QUARTERS, 2...  33.8 us
    pallas_call x1, Pallas kernels, finish(): pl.pallas_call(finish_kernel, out_shape=tuple((jax.ShapeDtypeStruct(shape...  1.7 us

profile of v7, /device:TPU:7, one launch (start us, length us, event | category | flops | bytes accessed | tf_op | source)
XLA Modules:
  0.0 36.2 jit_solution(2607215131853962187)
XLA Ops:
  0.6 33.8 %sweep.1 = (f32[4,2,32,128]{3,2,1,0:T(8,128)S(1)}, f32[32,128,128]{2,1,0:T(8,128)S(1)}) custom-call(s32[64]{0:T(128)} %parents_hbm.1, s32[64]{0:T(128)} %kinds_hbm.1, s32[1,64]{1,0:T(1,128)} %bitcast.7, f32[32,128,128]{2,1,0:T(8,128)} %bitcast.5, f32[32,128]{1,0:T(8,128)} %bitcast.6), custom_call_target="tpu_custom_call" | custom-call | tf_op jit(solution)/shard_map/sweep/pallas_call | solution.py:460
  34.5 1.7 %finish.1 = (f32[32,128]{1,0:T(8,128)}, f32[32,128,128]{2,1,0:T(8,128)}) custom-call(f32[4,2,32,128]{3,2,1,0:T(8,128)S(1)} %get-tuple-element.6.final, f32[32,128,128]{2,1,0:T(8,128)S(1)} %get-tuple-element.7.pot), custom_call_target="tpu_custom_call" | custom-call | tf_op jit(solution)/shard_map/finish/pallas_call | solution.py:509

commit v8 on v7

--- a/solution.py
+++ b/solution.py
@@ -486,11 +486,11 @@
     me = lax.axis_index("wide")
     quarter = lax.axis_index("narrow")
     cells = final[:, 0]
-    largest = jnp.max(cells)
+    largest = jnp.max(cells, axis=(0, 1, 2), keepdims=True)
     weights = jnp.exp(cells - largest)
-    scale = jnp.float32(K * K) / jnp.sum(weights)
+    scale = jnp.float32(K * K) / jnp.sum(weights, axis=(0, 1, 2), keepdims=True)
     whole = weights * scale
-    marginal[...] = jnp.exp(final[quarter, 0] - largest) * scale
+    marginal[...] = jnp.exp(final[quarter, 0] - largest[0]) * scale[0]
     copies = [pltpu.make_async_copy(marginal, marginal_hbm, sem.at[0])]
     copies[0].start()
     term = jnp.where(me >= LEVEL2, jnp.float32(0.5) * (whole - final[:, 1]), jnp.float32(0.0)).reshape(K, K)

time: 36.3 us -> 36.2 us (level)
  no operation moved by 1% of the time
where the time goes in v8:
time: 36.2 us; the launch traced here: 36.1 us
  Pallas kernels  35.5 us (98%)
  between operations  0.64 us (2%)
    pallas_call x1, Pallas kernels, sweep(): pl.pallas_call(sweep_kernel, out_shape=(jax.ShapeDtypeStruct((QUARTERS, 2...  33.8 us
    pallas_call x1, Pallas kernels, finish(): pl.pallas_call(finish_kernel, out_shape=tuple((jax.ShapeDtypeStruct(shape...  1.67 us

profile of v8, /device:TPU:7, one launch (start us, length us, event | category | flops | bytes accessed | tf_op | source)
XLA Modules:
  0.0 36.1 jit_solution(6980376922180026419)
XLA Ops:
  0.6 33.8 %sweep.1 = (f32[4,2,32,128]{3,2,1,0:T(8,128)S(1)}, f32[32,128,128]{2,1,0:T(8,128)S(1)}) custom-call(s32[64]{0:T(128)} %parents_hbm.1, s32[64]{0:T(128)} %kinds_hbm.1, s32[1,64]{1,0:T(1,128)} %bitcast.7, f32[32,128,128]{2,1,0:T(8,128)} %bitcast.5, f32[32,128]{1,0:T(8,128)} %bitcast.6), custom_call_target="tpu_custom_call" | custom-call | tf_op jit(solution)/shard_map/sweep/pallas_call | solution.py:460
  34.5 1.7 %finish.1 = (f32[32,128]{1,0:T(8,128)}, f32[32,128,128]{2,1,0:T(8,128)}) custom-call(f32[4,2,32,128]{3,2,1,0:T(8,128)S(1)} %get-tuple-element.6.final, f32[32,128,128]{2,1,0:T(8,128)S(1)} %get-tuple-element.7.pot), custom_call_target="tpu_custom_call" | custom-call | tf_op jit(solution)/shard_map/finish/pallas_call | solution.py:509
